TPU v7x, 32 devices: a whole 2x2x4 slice. The times are simulated.
32 devices in a mesh: groups: 2 (over x), hidden: 4 (over y, core), mp: 4 (over z).
Axes of the slice: x: 2, y: 2, z: 4, core: 2. Of those that a mesh axis runs over, the one named last changes fastest.
Arguments:
- tokens: bfloat16 [256, 8192], P(('groups', 'hidden'), 'mp'), parts along dimension 0, may hold values from -6 to 6
- up_codes: bfloat16 [8192, 24576], P('mp', 'hidden'), may hold values from -0.0625 to 0.0625
- up_scales: float32 [64, 192], P('mp', 'hidden'), may hold values from 0.5 to 2
- up_bias: bfloat16 [24576], P('hidden'), may hold values from -3 to 3
- down_codes: bfloat16 [24576, 8192], P('hidden', 'mp'), may hold values from -0.0390625 to 0.0390625
- down_scales: float32 [192, 64], P('hidden', 'mp'), may hold values from 0.5 to 2
- down_bias: bfloat16 [8192], P('mp'), may hold values from -3 to 3
- cotangent: bfloat16 [256, 8192], P(('groups', 'hidden'), 'mp'), parts along dimension 0, may hold values from -6 to 6
Outputs:
- ffn_output: bfloat16 [256, 8192], P(('groups', 'hidden'), 'mp'), parts along dimension 0
- grad_tokens: bfloat16 [256, 8192], P(('groups', 'hidden'), 'mp'), parts along dimension 0
- grad_up: bfloat16 [16384, 24576], P(('groups', 'mp'), 'hidden'), parts along dimension 0
- grad_down: bfloat16 [49152, 8192], P(('groups', 'hidden'), 'mp'), parts along dimension 0
- grad_up_bias: float32 [49152], P(('groups', 'hidden')), parts along dimension 0
There are 2 independent parts, one for each index of `groups`. A program takes and returns all parts, laid end to end along the dimension named above; an argument that names none is the same for every part. Nothing has to cross between parts.
All inputs are finite; a program needn't handle non-finite values.
Results may differ from a plain program's by a relative error of at most 0.017.
Values may be sent and summed in bfloat16 or wider, within the bound.
No kernel may reach another device: no remote copies, remote signals or barrier semaphores. Data moves between devices by JAX's collectives and lax.ppermute only.
A program may use at most 384 MiB of HBM per device.

v0:
```python
import functools

import jax
import jax.numpy as jnp
from jax import lax
from jax.experimental import pallas as pl
from jax.experimental.pallas import tpu as pltpu
from jax.sharding import PartitionSpec as P

root_two_pi = 0.7978845608028654
cubic_coef = 0.044715
LANES = 128
MIB = 1024 * 1024
COST_SCALE = 3
SHARE_MIB = 4
GRADIENT_MIB = 12
DOWN_UNROLL = 3
GRADIENT_UNROLL = 2
KEEP_UP = (0, 3)
KEEP_DOWN = (0, 3)


def gelu_value(argument):
    inner_arg = root_two_pi * (argument + cubic_coef * argument * argument * argument)
    return 0.5 * argument * (1.0 + jnp.tanh(inner_arg))


def gelu_slope(argument):
    inner_arg = root_two_pi * (argument + cubic_coef * argument * argument * argument)
    tangent = jnp.tanh(inner_arg)
    return 0.5 * (1.0 + tangent) + 0.5 * argument * (1.0 - tangent * tangent) * root_two_pi * (
        1.0 + 3.0 * cubic_coef * argument * argument
    )


def dequantize(weight_codes, block_scales):
    row_count, col_count = weight_codes.shape
    scale_rows, scale_cols = block_scales.shape
    blocks = weight_codes.astype(jnp.float32).reshape(
        scale_rows, row_count // scale_rows, scale_cols, col_count // scale_cols
    )
    scaled = blocks * block_scales[:, None, :, None]
    return scaled.reshape(row_count, col_count).astype(jnp.bfloat16)


def plain_product(left_side, right_side):
    return jnp.dot(left_side, right_side, preferred_element_type=jnp.float32)


def product_transposed(left_side, right_side):
    return lax.dot_general(
        left_side, right_side, (((1,), (1,)), ((), ())), preferred_element_type=jnp.float32
    )


def transposed_product(left_side, right_side):
    return lax.dot_general(
        left_side, right_side, (((0,), (0,)), ((), ())), preferred_element_type=jnp.float32
    )


def span(first, count):
    return pl.ds(pl.multiple_of(first, LANES), count)


def up_scaled(side, weights_ref, scales_ref, block, first, count):
    columns = span(first, count)
    scale_columns = span(block * weights_ref.shape[1] + first, count)
    for row in range(weights_ref.shape[0] // side):
        rows = slice(row * side, (row + 1) * side)
        weights_ref[rows, columns] = (
            weights_ref[rows, columns].astype(jnp.float32) * scales_ref[row : row + 1, scale_columns]
        ).astype(jnp.bfloat16)
    return weights_ref[:, columns]


def down_scaled(side, weights_ref, scales_ref, block, first, count):
    for row in range(count // side):
        rows = span(first + row * side, side)
        weights_ref[rows, :] = (
            weights_ref[rows, :].astype(jnp.float32)
            * scales_ref[block, pl.ds(first // side + row, 1), :]
        ).astype(jnp.bfloat16)
    return weights_ref[span(first, count), :]


def code_copy(up, piece, codes_ref, weights_ref, sems, block, index):
    block_width = weights_ref.shape[1 if up else 0]
    there = span(block * block_width + index * piece, piece)
    here = span(index * piece, piece)
    return pltpu.make_async_copy(
        codes_ref.at[:, there] if up else codes_ref.at[there, :],
        weights_ref.at[:, here] if up else weights_ref.at[here, :],
        sems.at[index],
    )


def each(count, body, unroll=1):
    def step(index, nothing):
        body(index)
        return nothing

    lax.fori_loop(0, count, step, None, unroll=unroll)


def share_kernel(side, up, piece, part_count, sum_in, turn, block_ref, *refs):
    refs = list(refs)
    block = block_ref[0]
    parts = [refs.pop(0) for _ in range(part_count)]
    rows_ref = None if part_count else refs.pop(0)
    codes_ref, scales_ref = refs.pop(0), refs.pop(0)
    sum_ref = refs.pop(0) if sum_in else None
    out_ref = refs.pop(0)
    if part_count:
        rows_ref = refs.pop(0)
    turned_ref = refs.pop(0) if turn else None
    weights_ref, sems = refs.pop(0), refs.pop(0)
    sum_held = refs.pop(0) if sum_in else None
    count = out_ref.shape[1] // piece

    def copy(index):
        return code_copy(up, piece, codes_ref, weights_ref, sems, block, index)

    if part_count:
        depth = parts[0].shape[0]
        own_copy = pltpu.make_async_copy(parts[0], rows_ref.at[:depth, :], sems.at[count])
        own_copy.start()
    if sum_in:
        sum_copy = pltpu.make_async_copy(sum_ref, sum_held, sems.at[count])
        sum_copy.start()
    each(count, lambda index: copy(index).start())
    if part_count:
        for index, part in enumerate(parts):
            if index == 0:
                continue
            rows_ref[index * depth : (index + 1) * depth, :] = part[...]
        own_copy.wait()
    if turn:
        turned_ref[...] = rows_ref[...].T
    if sum_in:
        sum_copy.wait()

    def work(index):
        copy(index).wait()
        columns = span(index * piece, piece)
        if up:
            weights = up_scaled(side, weights_ref, scales_ref, block, index * piece, piece)
            share = plain_product(rows_ref[...], weights)
        else:
            weights = down_scaled(side, weights_ref, scales_ref, block, index * piece, piece)
            share = product_transposed(rows_ref[...], weights)
        if sum_in:
            share = share.astype(jnp.bfloat16).astype(jnp.float32) + sum_held[:, columns].astype(
                jnp.float32
            )
        out_ref[:, columns] = share.astype(jnp.bfloat16)

    each(count, work, 1 if up else DOWN_UNROLL)


def activation_kernel(sum_ref, share_ref, bias_ref, act_ref, slope_ref):
    preact = (
        sum_ref[...].astype(jnp.float32)
        + share_ref[...].astype(jnp.float32)
        + bias_ref[...].astype(jnp.float32)
    )
    act_ref[...] = gelu_value(preact).astype(jnp.bfloat16)
    slope_ref[...] = gelu_slope(preact)


def product_kernel(act_ref, weights_ref, total_in, after_ref, kept_ref, sent_ref):
    total = (total_in[...] + product_transposed(weights_ref[...], act_ref[...])).T
    half = total.shape[0] // 2
    kept_ref[...] = total[:half, :]
    sent_ref[...] = total[half:, :].astype(jnp.bfloat16)


def gradient_kernel(side, up, piece, fresh, last, kept_weights, summed, block_ref, *refs):
    refs = list(refs)
    block = block_ref[0]
    block_act, rows_ref = refs.pop(0), refs.pop(0)
    weights_ref = refs.pop(0) if kept_weights and summed else None
    codes_ref, scales_ref = (None, None) if kept_weights else (refs.pop(0), refs.pop(0))
    if not fresh:
        total_in = refs.pop(0) if summed else None
        refs.pop(0)
        bias_in = refs.pop(0) if up else None
    refs.pop(0)
    if last and summed:
        kept_ref, sent_ref = refs.pop(0), refs.pop(0)
    elif summed:
        total_ref = refs.pop(0)
    grad_ref = refs.pop(0)
    bias_ref = refs.pop(0) if up else None
    if last and summed:
        total_ref = refs.pop(0)
    staged, out_sems = refs.pop(0), refs.pop(0)
    block_width = block_act.shape[1]
    count = block_width // piece

    def copy(index):
        return code_copy(up, piece, codes_ref, weights_ref, sems, block, index)

    def write(index):
        there = span(block * block_width + index * piece, piece)
        return pltpu.make_async_copy(
            staged.at[index], grad_ref.at[:, there] if up else grad_ref.at[there, :], out_sems.at[index]
        )

    if not kept_weights:
        weights_ref, sems = refs
        each(count, lambda index: copy(index).start())
    if up and not fresh:
        bias_ref[...] = bias_in[...]
    if summed:
        total_ref[...] = jnp.zeros_like(total_ref) if fresh else total_in[...]

    def work(index):
        columns = span(index * piece, piece)
        act = block_act[:, columns]
        if up:
            gradient = plain_product(rows_ref[...], act)
            bias_ref[0:1, span(block * block_width + index * piece, piece)] = jnp.sum(
                act.astype(jnp.float32), axis=0, keepdims=True
            )
        else:
            gradient = transposed_product(act, rows_ref[...])
        staged[index] = gradient.astype(jnp.bfloat16)
        write(index).start()
        if not summed:
            return
        if not kept_weights:
            copy(index).wait()
            scaled = up_scaled if up else down_scaled
            scaled(side, weights_ref, scales_ref, block, index * piece, piece)
        if up:
            total_ref[...] += product_transposed(weights_ref[:, columns], act)
        else:
            total_ref[...] += plain_product(act, weights_ref[columns, :])

    each(count, work, GRADIENT_UNROLL)
    if last and summed:
        half = total_ref.shape[0] // 2
        kept_ref[...] = total_ref[:half, :]
        sent_ref[...] = total_ref[half:, :].astype(jnp.bfloat16)
    each(count, lambda index: write(index).wait())


def cost_of(token_count, width, hidden_count, products, passes):
    return pl.CostEstimate(
        flops=COST_SCALE * 2 * products * token_count * width * hidden_count,
        bytes_accessed=COST_SCALE * 2 * passes * width * hidden_count,
        transcendentals=0,
    )


ANY_SPEC = pl.BlockSpec(memory_space=pl.ANY)
VMEM_SPEC = pl.BlockSpec(memory_space=pltpu.VMEM)
SMEM_SPEC = pl.BlockSpec(memory_space=pltpu.SMEM)


class Operands:
    def __init__(self, block):
        self.arrays, self.specs = [block], [SMEM_SPEC]

    def add(self, array, spec=VMEM_SPEC):
        self.arrays.append(array)
        self.specs.append(spec)


def call(name, kernel, operands, outs, scratch, cost, limit, aliases=None):
    return pl.pallas_call(
        kernel,
        in_specs=operands.specs,
        out_specs=[spec for _, spec in outs],
        scratch_shapes=scratch,
        out_shape=[shape for shape, _ in outs],
        input_output_aliases=aliases or {},
        cost_estimate=cost,
        name=name,
        compiler_params=pltpu.CompilerParams(vmem_limit_bytes=limit * MIB),
    )(*operands.arrays)


class Sizes:
    def __init__(self, rows, width, hidden, block_width, side):
        self.rows, self.width, self.hidden = rows, width, hidden
        self.block_width, self.side = block_width, side

    def piece(self, most):
        return next(
            size for size in (512, 256, 128) if size <= most and self.block_width % size == 0
        )

    def weights_shape(self, up):
        return (self.width, self.block_width) if up else (self.block_width, self.width)


def share_call(sizes, up, block, rows, codes, scales, sum_in, keep, turn=False):
    parts = rows if isinstance(rows, list) else []
    operands = Operands(block)
    for index, part in enumerate(parts or [rows]):
        if parts and index == 0:
            operands.add(pltpu.with_memory_space_constraint(part, pltpu.HBM), ANY_SPEC)
        else:
            operands.add(part)
    operands.add(pltpu.with_memory_space_constraint(codes, pltpu.HBM), ANY_SPEC)
    operands.add(scales)
    if sum_in is not None:
        operands.add(sum_in, ANY_SPEC)
    outs = [(pltpu.VMEM((sizes.rows, sizes.block_width), jnp.bfloat16), VMEM_SPEC)]
    if parts:
        outs.append((jax.ShapeDtypeStruct((sizes.rows, sizes.width), jnp.bfloat16), VMEM_SPEC))
    if turn:
        outs.append((jax.ShapeDtypeStruct((sizes.width, sizes.rows), jnp.bfloat16), VMEM_SPEC))
    weights = pltpu.VMEM(sizes.weights_shape(up), jnp.bfloat16)
    if keep:
        outs.append((weights, VMEM_SPEC))
    piece = sizes.piece(256 if up else 512)
    return call(
        "up_share" if up else "down_share",
        functools.partial(share_kernel, sizes.side, up, piece, len(parts), sum_in is not None, turn),
        operands,
        outs,
        ([] if keep else [weights])
        + [pltpu.SemaphoreType.DMA((sizes.block_width // piece + 1,))]
        + ([] if sum_in is None else [pltpu.VMEM((sizes.rows, sizes.block_width), jnp.bfloat16)]),
        cost_of(sizes.rows, sizes.width, sizes.block_width, 1, 1),
        SHARE_MIB if keep else SHARE_MIB + 7,
    )


def gradient_call(
    sizes, up, block, block_act, rows, weights, codes, scales, held, after, last, summed=True
):
    full_shape = (sizes.width, sizes.rows) if up else (sizes.rows, sizes.width)
    half_shape = (sizes.rows // 2, sizes.width)
    kept = weights is not None
    operands = Operands(block)
    operands.add(block_act)
    operands.add(rows)
    if kept and summed:
        operands.add(pltpu.with_memory_space_constraint(weights, pltpu.VMEM))
    elif not kept:
        operands.add(pltpu.with_memory_space_constraint(codes, pltpu.HBM), ANY_SPEC)
        operands.add(scales)
    fresh = held is None
    aliases = {}
    if not fresh:
        at = len(operands.arrays)
        if summed:
            aliases = {at + 1: 2 if last else 1}
            operands.add(held[0])
        else:
            aliases = {at: 0}
        operands.add(pltpu.with_memory_space_constraint(held[1], pltpu.HBM), ANY_SPEC)
        if up:
            operands.add(held[2])
    operands.add(after, ANY_SPEC)
    if not summed:
        outs = []
    elif last:
        outs = [
            (jax.ShapeDtypeStruct(half_shape, jnp.float32), VMEM_SPEC),
            (jax.ShapeDtypeStruct(half_shape, jnp.bfloat16), VMEM_SPEC),
        ]
    else:
        outs = [(jax.ShapeDtypeStruct(full_shape, jnp.float32), VMEM_SPEC)]
    outs.append((pltpu.HBM(codes.shape, jnp.bfloat16), ANY_SPEC))
    if up:
        outs.append((jax.ShapeDtypeStruct((1, sizes.hidden), jnp.float32), VMEM_SPEC))
    piece = sizes.piece(256)
    slot_shape = (sizes.width, piece) if up else (piece, sizes.width)
    slots = sizes.block_width // piece
    scratch = [pltpu.VMEM(full_shape, jnp.float32)] if last and summed else []
    scratch += [pltpu.VMEM((slots,) + slot_shape, jnp.bfloat16), pltpu.SemaphoreType.DMA((slots,))]
    if not kept:
        scratch += [
            pltpu.VMEM(sizes.weights_shape(up), jnp.bfloat16),
            pltpu.SemaphoreType.DMA((sizes.block_width // piece,)),
        ]
    return call(
        "up_gradient" if up else "down_gradient",
        functools.partial(gradient_kernel, sizes.side, up, piece, fresh, last, kept, summed),
        operands,
        outs,
        scratch,
        cost_of(sizes.rows, sizes.width, sizes.block_width, 2, 2 if summed else 1),
        GRADIENT_MIB if kept else GRADIENT_MIB + 7,
        aliases,
    )


def activation_call(sizes, sum_in, share, bias):
    block_shape = (sizes.rows, sizes.block_width)
    return pl.pallas_call(
        activation_kernel,
        in_specs=[VMEM_SPEC] * 3,
        out_specs=[VMEM_SPEC] * 2,
        out_shape=[
            jax.ShapeDtypeStruct(block_shape, jnp.bfloat16),
            jax.ShapeDtypeStruct(block_shape, jnp.float32),
        ],
        name="activation",
        compiler_params=pltpu.CompilerParams(vmem_limit_bytes=SHARE_MIB * MIB),
    )(sum_in, share, bias)


def product_call(sizes, block_act, weights, total_in, after):
    half_shape = (sizes.rows // 2, sizes.width)
    return pl.pallas_call(
        product_kernel,
        in_specs=[VMEM_SPEC] * 3 + [ANY_SPEC],
        out_specs=[VMEM_SPEC] * 2,
        out_shape=[
            jax.ShapeDtypeStruct(half_shape, jnp.float32),
            jax.ShapeDtypeStruct(half_shape, jnp.bfloat16),
        ],
        cost_estimate=cost_of(sizes.rows, sizes.width, sizes.block_width, 1, 1),
        name="last_product",
        compiler_params=pltpu.CompilerParams(vmem_limit_bytes=SHARE_MIB * MIB),
    )(block_act, pltpu.with_memory_space_constraint(weights, pltpu.VMEM), total_in, after)


def ring_program(mp_count, hidden_count):
    ring = [(i, (i + 1) % mp_count) for i in range(mp_count)]
    bits = [1 << bit for bit in reversed(range(hidden_count.bit_length() - 1))]

    def partner_pairs(bit):
        return [(i, i ^ bit) for i in range(hidden_count)]

    def after(array, *earlier):
        return lax.optimization_barrier((array, *earlier))[0]

    def first_exchange(own_rows):
        return [own_rows, lax.ppermute(own_rows, "hidden", partner_pairs(bits[0]))]

    def later_exchanges(held, *earlier):
        held = [held[0], after(held[1], *earlier)] if earlier else held
        for bit in bits[1:]:
            held = held + [lax.ppermute(part, "hidden", partner_pairs(bit)) for part in held]
        return held

    def scattered_sum(kept, sent):
        for bit in reversed(bits):
            kept = kept + lax.ppermute(sent, "hidden", partner_pairs(bit)).astype(jnp.float32)
            half = kept.shape[0] // 2
            if bit != bits[0]:
                kept, sent = kept[:half], kept[half:].astype(jnp.bfloat16)
        return kept, sent

    def passed_on(block):
        return lax.ppermute(block, "mp", ring)

    def added(left, right):
        return left.astype(jnp.float32) + right.astype(jnp.float32)

    def on_device(
        tokens, up_codes, up_scales, up_bias, down_codes, down_scales, down_bias, cotangent
    ):
        width, hidden = up_codes.shape
        side = width // up_scales.shape[0]
        block_width = hidden // mp_count
        sizes = Sizes(tokens.shape[0] * hidden_count, width, hidden, block_width, side)
        me = lax.axis_index("mp").astype(jnp.int32)

        up_wide = jnp.repeat(up_scales, side, axis=1)
        down_wide = jnp.repeat(down_scales, side, axis=1).reshape(mp_count, -1, width)
        token_rows = first_exchange(tokens)
        cot_rows = first_exchange(after(cotangent, token_rows[1]))
        own_bias = lax.dynamic_slice(
            up_bias.reshape(1, hidden), (0, me * block_width), (1, block_width)
        )
        token_rows = later_exchanges(token_rows, up_wide, down_wide, own_bias)

        def block_number(back):
            return ((me + 2 * mp_count - back) % mp_count).reshape(1)

        up_weights, down_weights = {}, {}

        def up_share(back, rows, sum_in, turn, *earlier):
            block = after(block_number(back), *earlier)
            made = share_call(
                sizes, True, block, rows, up_codes, up_wide, sum_in, back in KEEP_UP, turn
            )
            if back in KEEP_UP:
                up_weights[back] = made[-1]
            return made

        def down_share(back, rows, sum_in, *earlier):
            block = after(block_number(back), *earlier)
            made = share_call(
                sizes, False, block, rows, down_codes, down_wide, sum_in, back in KEEP_DOWN
            )
            if back in KEEP_DOWN:
                down_weights[back] = made[-1]
            return made

        up_part, token_rows, *made = up_share(1, token_rows, None, mp_count == 2)
        turned_tokens = made[0] if mp_count == 2 else None
        up_sum = passed_on(up_part)
        down_part, cot_rows, *_ = down_share(1, later_exchanges(cot_rows, up_part), None)
        down_sum = passed_on(down_part)
        for back in range(2, mp_count):
            last = back == mp_count - 1
            up_part, *made = up_share(back, token_rows, up_sum, last)
            up_sum = passed_on(up_part)
            if last:
                turned_tokens = made[0]
                own_part = up_share(0, token_rows, None, False, up_part)[0]
            down_part = down_share(back, cot_rows, down_sum, *([own_part] if last else []))[0]
            down_sum = passed_on(down_part)
        if mp_count == 2:
            own_part = up_share(0, token_rows, None, False, up_part)[0]
        act_block, slope = activation_call(sizes, up_sum, own_part, own_bias)
        down_part = down_share(0, cot_rows, None, act_block)[0]
        pre_block = (added(down_sum, down_part) * slope).astype(jnp.bfloat16)

        output_held = input_held = None
        for back in range(mp_count):
            last = back == mp_count - 1
            sent_act = act_block if back == 0 else after(act_block, input_held[0])
            next_act = None if last else passed_on(sent_act)
            output_held = gradient_call(
                sizes, False, block_number(back), act_block, cot_rows, down_weights.get(back),
                down_codes, down_wide, output_held,
                pre_block if back == 0 else input_held[0], last,
            )
            sent_pre = pre_block if back == 0 else after(pre_block, output_held[0])
            next_pre = None if last else passed_on(sent_pre)
            if last:
                output_sum, output_sent = scattered_sum(output_held[0], output_held[1])
                tokens_kept, tokens_sent = product_call(
                    sizes, pre_block, up_weights[back], input_held[0], output_held[1]
                )
                tokens_sum, tokens_sent = scattered_sum(tokens_kept, tokens_sent)
                ordering = after(tokens_sent, output_sent)
            else:
                ordering = output_held[0]
            input_held = gradient_call(
                sizes, True, block_number(back), pre_block, turned_tokens, up_weights.get(back),
                up_codes, up_wide, input_held, ordering, last, not last,
            )
            act_block, pre_block = next_act, next_pre
        grad_down = output_held[-1]
        grad_up, grad_up_bias = input_held
        ffn_output = (output_sum + down_bias.astype(jnp.float32)).astype(jnp.bfloat16)
        grad_tokens = tokens_sum.astype(jnp.bfloat16)
        return (ffn_output, grad_tokens, grad_up, grad_down, grad_up_bias.reshape(hidden))

    return on_device


def plain_program(
    tokens, up_codes, up_scales, up_bias, down_codes, down_scales, down_bias, cotangent
):
    w_up = dequantize(up_codes, up_scales)
    w_down = dequantize(down_codes, down_scales)
    cot_rows = lax.all_gather(cotangent, "hidden", axis=0, tiled=True)
    token_rows = lax.all_gather(tokens, "hidden", axis=0, tiled=True)
    bias_up = up_bias.astype(jnp.float32)

    def summed(share, axis):
        return lax.psum_scatter(
            share.astype(jnp.bfloat16), axis, scatter_dimension=0, tiled=True
        ).astype(jnp.float32)

    preact_share = summed(plain_product(token_rows, w_up), "mp") + bias_up
    act_share = gelu_value(preact_share).astype(jnp.bfloat16)
    act_rows = lax.all_gather(act_share, "mp", axis=0, tiled=True)
    grad_share = summed(product_transposed(cot_rows, w_down), "mp")
    grad_pre_share = (grad_share * gelu_slope(preact_share)).astype(jnp.bfloat16)
    grad_pre_rows = lax.all_gather(grad_pre_share, "mp", axis=0, tiled=True)
    output_sum = summed(plain_product(act_rows, w_down), "hidden")
    ffn_output = (output_sum + down_bias.astype(jnp.float32)).astype(jnp.bfloat16)
    grad_tokens = summed(product_transposed(grad_pre_rows, w_up), "hidden").astype(jnp.bfloat16)
    grad_up_bias = jnp.sum(grad_pre_rows, axis=0, dtype=jnp.float32)
    grad_down = transposed_product(act_rows, cot_rows).astype(jnp.bfloat16)
    grad_up = transposed_product(token_rows, grad_pre_rows).astype(jnp.bfloat16)
    return (ffn_output, grad_tokens, grad_up, grad_down, grad_up_bias)


def solution(mesh):
    mp_count, hidden_count = mesh.shape["mp"], mesh.shape["hidden"]

    def on_device(*arrays):
        hidden = arrays[1].shape[1]
        whole_blocks = hidden % (mp_count * LANES) == 0
        if whole_blocks and mp_count > 1 and hidden_count & (hidden_count - 1) == 0:
            return ring_program(mp_count, hidden_count)(*arrays)
        return plain_program(*arrays)

    in_specs = (
        P(("groups", "hidden"), "mp"),
        P("mp", "hidden"),
        P("mp", "hidden"),
        P("hidden"),
        P("hidden", "mp"),
        P("hidden", "mp"),
        P("mp"),
        P(("groups", "hidden"), "mp"),
    )
    out_specs = (
        P(("groups", "hidden"), "mp"),
        P(("groups", "hidden"), "mp"),
        P(("groups", "mp"), "hidden"),
        P(("groups", "hidden"), "mp"),
        P(("groups", "hidden")),
    )
    return jax.shard_map(
        on_device, mesh=mesh, in_specs=in_specs, out_specs=out_specs, check_vma=False
    )
```

profile of v0, /device:TPU:0, one launch (start us, length us, event | category | flops | bytes accessed | tf_op | source)
XLA Modules:
  0.0 130.6 jit_solution(13274621279498713005)
XLA Ops:
  0.6 0.0 copy-start
  0.6 3.0 %collective-permute-start = (bf16[32,2048]{1,0:T(8,128)(2,1)}, bf16[32,2048]{1,0:T(8,128)(2,1)S(1)}, u32[]{:S(2)}, u32[]{:S(2)}) collective-permute-start(bf16[32,2048]{1,0:T(8,128)(2,1)} %refs_0_.1), channel_id=1, source_target_pairs={{0,8},{4,12},{8,0},{12,4},{1,9},{5,13},{9,1},{13,5},{2,10},{6,14},... | collective-permute-start | bytes 393224 | tf_op jit(solution)/shard_map/ppermute | solution.py:436
  3.7 0.0 collective-permute-start.1
  3.7 0.8 dynamic-slice.3
  4.5 0.8 copy.20
  5.2 0.2 broadcast_in_dim.8
  5.4 0.1 reshape_reshape.3.refs_5_.refs_2_.refs_3_
  5.5 0.9 broadcast_in_dim.7
  6.3 0.1 copy.23
  6.5 0.9 collective-permute-done.refs_1_
  7.4 1.7 %collective-permute-start.7 = (bf16[32,2048]{1,0:T(8,128)(2,1)}, bf16[32,2048]{1,0:T(8,128)(2,1)S(1)}, u32[]{:S(2)}, u32[]{:S(2)}) collective-permute-start(bf16[32,2048]{1,0:T(8,128)(2,1)} %refs_0_.2), channel_id=1, source_target_pairs={{0,8},{4,12},{8,0},{12,4},{1,9},{5,13},{9,1},{13,5},{2,10},{6,14},... | collective-permute-start | bytes 393224 | tf_op jit(solution)/shard_map/ppermute | solution.py:436
  9.1 0.0 collective-permute-done.1.refs_2_
  9.1 0.0 collective-permute-done.2.refs_3_
  9.1 3.7 %up_share.4 = (bf16[128,1536]{1,0:T(8,128)(2,1)S(1)}, bf16[128,2048]{1,0:T(8,128)(2,1)S(1)}) custom-call(s32[1]{0:T(128)} %bitcast.1.block_ref, bf16[32,2048]{1,0:T(8,128)(2,1)} %refs_0_.1, bf16[32,2048]{1,0:T(8,128)(2,1)S(1)} %collective-permute-done.refs_1_, bf16[32,2048]{1,0:T(8,128)(2,1)S(1)} %collective-permute-done.1.refs_2_, ...), custom_call_target="tpu_custom_call" | custom-call | flops 2415919104 | bytes 18874368 | tf_op jit(solution)/shard_map/up_share/pallas_call | solution.py:272
  12.9 1.6 %collective-permute-start.3 = (bf16[128,1536]{1,0:T(8,128)(2,1)S(1)}, bf16[128,1536]{1,0:T(8,128)(2,1)S(1)}, u32[]{:S(2)}, u32[]{:S(2)}) collective-permute-start(bf16[128,1536]{1,0:T(8,128)(2,1)S(1)} %get-tuple-element.55), channel_id=1, source_target_pairs={{0,1},{1,2},{2,3},{3,0},{4,5},{5,6},{6,7},{7,4},{8,9},{9,10},{10,1... | collective-permute-start | bytes 1179656 | tf_op jit(solution)/shard_map/ppermute | solution.py:453
  14.5 0.5 collective-permute-start.9
  15.0 0.8 collective-permute-done.8.refs_2_
  15.8 0.2 collective-permute-done.9.refs_3_
  16.0 4.4 %down_share.4 = (bf16[128,1536]{1,0:T(8,128)(2,1)S(1)}, bf16[128,2048]{1,0:T(8,128)(2,1)S(1)}) custom-call(s32[1]{0:T(128)} %bitcast.1.block_ref, bf16[32,2048]{1,0:T(8,128)(2,1)} %refs_0_.2, bf16[32,2048]{1,0:T(8,128)(2,1)S(1)} %collective-permute-done.7.refs_1_, bf16[32,2048]{1,0:T(8,128)(2,1)S(1)} %collective-permute-done.8.refs_2_, ...), custom_call_target="tpu_custom_call" | custom-call | flops 2415919104 | bytes 18874368 | tf_op jit(solution)/shard_map/down_share/pallas_call | solution.py:272
  20.5 1.6 %collective-permute-start.10 = (bf16[128,1536]{1,0:T(8,128)(2,1)S(1)}, bf16[128,1536]{1,0:T(8,128)(2,1)S(1)}, u32[]{:S(2)}, u32[]{:S(2)}) collective-permute-start(bf16[128,1536]{1,0:T(8,128)(2,1)S(1)} %get-tuple-element.64), channel_id=1, source_target_pairs={{0,1},{1,2},{2,3},{3,0},{4,5},{5,6},{6,7},{7,4},{8,9},{9,10},{10,1... | collective-permute-start | bytes 1179656 | tf_op jit(solution)/shard_map/ppermute | solution.py:453
  22.1 4.5 %collective-permute-done.3.refs_3_ = bf16[128,1536]{1,0:T(8,128)(2,1)S(1)} collective-permute-done((bf16[128,1536]{1,0:T(8,128)(2,1)S(1)}, bf16[128,1536]{1,0:T(8,128)(2,1)S(1)}, u32[]{:S(2)}, u32[]{:S(2)}) %collective-permute-start.3) | collective-permute-done | bytes 393248 | tf_op jit(solution)/shard_map/ppermute | solution.py:453
  26.6 3.8 %up_share.5 = bf16[128,1536]{1,0:T(8,128)(2,1)S(1)} custom-call(s32[1]{0:T(128)} %bitcast.2.block_ref, bf16[128,2048]{1,0:T(8,128)(2,1)S(1)} %get-tuple-element.54.refs_0_, bf16[2048,6144]{1,0:T(8,128)(2,1)} %refs_2_.7, f32[16,6144]{1,0:T(8,128)S(1)} %bitcast.10, bf16[128,1536]{1,0:T(8,128)(2,1)S(1)} %collective-permute-done.3.refs_3_), custom_call_target="tpu_custom_call" | custom-call | flops 2415919104 | bytes 18874368 | tf_op jit(solution)/shard_map/up_share/pallas_call | solution.py:272
  30.5 0.1 collective-permute-start.4
  30.6 4.5 %collective-permute-done.10.refs_3_ = bf16[128,1536]{1,0:T(8,128)(2,1)S(1)} collective-permute-done((bf16[128,1536]{1,0:T(8,128)(2,1)S(1)}, bf16[128,1536]{1,0:T(8,128)(2,1)S(1)}, u32[]{:S(2)}, u32[]{:S(2)}) %collective-permute-start.10) | collective-permute-done | bytes 393248 | tf_op jit(solution)/shard_map/ppermute | solution.py:453
  35.1 4.6 %down_share.5 = bf16[128,1536]{1,0:T(8,128)(2,1)S(1)} custom-call(s32[1]{0:T(128)} %bitcast.2.block_ref, bf16[128,2048]{1,0:T(8,128)(2,1)S(1)} %get-tuple-element.63.refs_0_.refs_1_, bf16[6144,2048]{1,0:T(8,128)(2,1)} %refs_2_.6, f32[4,12,2048]{2,1,0:T(8,128)S(1)} %reshape_reshape.3.refs_5_.refs_2_.refs_3_, bf16[128,1536]{1,0:T(8,128)(2,1)S(1)} %collective-permute-done.10.refs_3_), custom_call_target="tpu_custom_call" | custom-call | flops 2415919104 | bytes 18874368 | tf_op jit(solution)/shard_map/down_share/pallas_call | solution.py:272
  39.6 0.1 collective-permute-start.11
  39.7 3.2 %collective-permute-done.4.refs_3_ = bf16[128,1536]{1,0:T(8,128)(2,1)S(1)} collective-permute-done((bf16[128,1536]{1,0:T(8,128)(2,1)S(1)}, bf16[128,1536]{1,0:T(8,128)(2,1)S(1)}, u32[]{:S(2)}, u32[]{:S(2)}) %collective-permute-start.4) | collective-permute-done | bytes 393248 | tf_op jit(solution)/shard_map/ppermute | solution.py:453
  42.9 3.8 %up_share.6 = (bf16[128,1536]{1,0:T(8,128)(2,1)S(1)}, bf16[2048,128]{1,0:T(8,128)(2,1)S(1)}, bf16[2048,1536]{1,0:T(8,128)(2,1)S(1)}) custom-call(s32[1]{0:T(128)} %bitcast.block_ref, bf16[128,2048]{1,0:T(8,128)(2,1)S(1)} %get-tuple-element.54.refs_0_, bf16[2048,6144]{1,0:T(8,128)(2,1)} %refs_2_.7, f32[16,6144]{1,0:T(8,128)S(1)} %bitcast.11, ...), custom_call_target="tpu_custom_call" | custom-call | flops 2415919104 | bytes 18874368 | tf_op jit(solution)/shard_map/up_share/pallas_call | solution.py:272
  46.7 0.4 collective-permute-start.5
  47.1 3.6 %up_share.7 = (bf16[128,1536]{1,0:T(8,128)(2,1)S(1)}, bf16[2048,1536]{1,0:T(8,128)(2,1)S(1)}) custom-call(s32[1]{0:T(128)} %bitcast.3.block_ref, bf16[128,2048]{1,0:T(8,128)(2,1)S(1)} %get-tuple-element.54.refs_0_, bf16[2048,6144]{1,0:T(8,128)(2,1)} %refs_2_.7, f32[16,6144]{1,0:T(8,128)S(1)} %bitcast.12), custom_call_target="tpu_custom_call" | custom-call | flops 2415919104 | bytes 18874368 | tf_op jit(solution)/shard_map/up_share/pallas_call | solution.py:272
  50.8 2.1 %collective-permute-done.11.refs_3_ = bf16[128,1536]{1,0:T(8,128)(2,1)S(1)} collective-permute-done((bf16[128,1536]{1,0:T(8,128)(2,1)S(1)}, bf16[128,1536]{1,0:T(8,128)(2,1)S(1)}, u32[]{:S(2)}, u32[]{:S(2)}) %collective-permute-start.11) | collective-permute-done | bytes 393248 | tf_op jit(solution)/shard_map/ppermute | solution.py:453
  52.9 4.6 %down_share.6 = (bf16[128,1536]{1,0:T(8,128)(2,1)S(1)}, bf16[1536,2048]{1,0:T(8,128)(2,1)S(1)}) custom-call(s32[1]{0:T(128)} %bitcast.block_ref, bf16[128,2048]{1,0:T(8,128)(2,1)S(1)} %get-tuple-element.63.refs_0_.refs_1_, bf16[6144,2048]{1,0:T(8,128)(2,1)} %refs_2_.6, f32[4,12,2048]{2,1,0:T(8,128)S(1)} %reshape_reshape.3.refs_5_.refs_2_.refs_3_, ...), custom_call_target="tpu_custom_call" | custom-call | flops 2415919104 | bytes 18874368 | tf_op jit(solution)/shard_map/down_share/pallas_call | solution.py:272
  57.5 0.1 collective-permute-start.12
  57.5 3.6 %collective-permute-done.5.sum_ref = bf16[128,1536]{1,0:T(8,128)(2,1)S(1)} collective-permute-done((bf16[128,1536]{1,0:T(8,128)(2,1)S(1)}, bf16[128,1536]{1,0:T(8,128)(2,1)S(1)}, u32[]{:S(2)}, u32[]{:S(2)}) %collective-permute-start.5) | collective-permute-done | bytes 393248 | tf_op jit(solution)/shard_map/ppermute | solution.py:453
  61.1 0.7 activation.1
  61.8 0.1 collective-permute-start.6
  61.9 4.3 %down_share.7 = (bf16[128,1536]{1,0:T(8,128)(2,1)S(1)}, bf16[1536,2048]{1,0:T(8,128)(2,1)S(1)}) custom-call(s32[1]{0:T(128)} %bitcast.3.block_ref, bf16[128,2048]{1,0:T(8,128)(2,1)S(1)} %get-tuple-element.63.refs_0_.refs_1_, bf16[6144,2048]{1,0:T(8,128)(2,1)} %refs_2_.6, f32[4,12,2048]{2,1,0:T(8,128)S(1)} %reshape_reshape.3.refs_5_.refs_2_.refs_3_), custom_call_target="tpu_custom_call" | custom-call | flops 2415919104 | bytes 18874368 | tf_op jit(solution)/shard_map/down_share/pallas_call | solution.py:272
  66.2 5.2 %collective-permute-done.12 = bf16[128,1536]{1,0:T(8,128)(2,1)S(1)} collective-permute-done((bf16[128,1536]{1,0:T(8,128)(2,1)S(1)}, bf16[128,1536]{1,0:T(8,128)(2,1)S(1)}, u32[]{:S(2)}, u32[]{:S(2)}) %collective-permute-start.12) | collective-permute-done | bytes 393248 | tf_op jit(solution)/shard_map/ppermute | solution.py:453
  71.4 0.1 multiply_convert_fusion.refs_3_.refs_0_
  71.5 0.2 collective-permute-start.14
  71.8 4.0 %down_gradient.4 = (f32[128,2048]{1,0:T(8,128)S(1)}, bf16[6144,2048]{1,0:T(8,128)(2,1)}) custom-call(s32[1]{0:T(128)} %bitcast.3.block_ref, bf16[128,1536]{1,0:T(8,128)(2,1)S(1)} %get-tuple-element.59.refs_0_, bf16[128,2048]{1,0:T(8,128)(2,1)S(1)} %get-tuple-element.63.refs_0_.refs_1_, bf16[1536,2048]{1,0:T(8,128)(2,1)S(1)} %get-tuple-element.71.refs_2_, ...), custom_call_target="tpu_custom_call" | custom-call | flops 4831838208 | bytes 37748736 | tf_op jit(solution)/shard_map/down_gradient/pallas_call | solution.py:272
  75.8 4.8 %up_gradient.4 = (f32[2048,128]{1,0:T(8,128)S(1)}, bf16[2048,6144]{1,0:T(8,128)(2,1)}, f32[1,6144]{1,0:T(1,128)S(1)}) custom-call(s32[1]{0:T(128)} %bitcast.3.block_ref, bf16[128,1536]{1,0:T(8,128)(2,1)S(1)} %multiply_convert_fusion.refs_3_.refs_0_, bf16[2048,128]{1,0:T(8,128)(2,1)S(1)} %get-tuple-element.69.refs_1_, ...), custom_call_target="tpu_custom_call" | custom-call | flops 4831838208 | bytes 37748736 | tf_op jit(solution)/shard_map/up_gradient/pallas_call | solution.py:272
  80.6 0.1 collective-permute-start.13
  80.7 7.3 %down_gradient.5 = (f32[128,2048]{1,0:T(8,128)S(1)}, bf16[6144,2048]{1,0:T(8,128)(2,1)}) custom-call(s32[1]{0:T(128)} %bitcast.1.block_ref, bf16[128,1536]{1,0:T(8,128)(2,1)S(1)} %collective-permute-done.6.refs_0_, bf16[128,2048]{1,0:T(8,128)(2,1)S(1)} %get-tuple-element.63.refs_0_.refs_1_, ...), custom_call_target="tpu_custom_call", output_to_operand_aliasing={{1}: (6, {})} | custom-call | flops 4831838208 | bytes 37748736 | tf_op jit(solution)/shard_map/down_gradient/pallas_call | solution.py:272
  88.0 0.2 collective-permute-done.14.refs_0_
  88.2 0.5 collective-permute-start.16
  88.7 7.1 %up_gradient.5 = (f32[2048,128]{1,0:T(8,128)S(1)}, bf16[2048,6144]{1,0:T(8,128)(2,1)}, f32[1,6144]{1,0:T(1,128)S(1)}) custom-call(s32[1]{0:T(128)} %bitcast.1.block_ref, bf16[128,1536]{1,0:T(8,128)(2,1)S(1)} %collective-permute-done.14.refs_0_, bf16[2048,128]{1,0:T(8,128)(2,1)S(1)} %get-tuple-element.69.refs_1_, ...), custom_call_target="tpu_custom_call", output_to_operand_aliasing={{1}: (6, {})} | custom-call | flops 4831838208 | bytes 37748736 | tf_op jit(solution)/shard_map/up_gradient/pallas_call | solution.py:272
  95.8 0.8 collective-permute-done.13.refs_0_
  96.7 3.5 %collective-permute-start.15 = (bf16[128,1536]{1,0:T(8,128)(2,1)S(1)}, bf16[128,1536]{1,0:T(8,128)(2,1)S(1)}, u32[]{:S(2)}, u32[]{:S(2)}) collective-permute-start(bf16[128,1536]{1,0:T(8,128)(2,1)S(1)} %collective-permute-done.13.refs_0_), channel_id=1, source_target_pairs={{0,1},{1,2},{2,3},{3,0},{4,5},{5,6},{6,7},{7,4},{8,9},{9,10},{10,1... | collective-permute-start | bytes 1179656 | tf_op jit(solution)/shard_map/ppermute | solution.py:453
  100.2 7.3 %down_gradient.6 = (f32[128,2048]{1,0:T(8,128)S(1)}, bf16[6144,2048]{1,0:T(8,128)(2,1)}) custom-call(s32[1]{0:T(128)} %bitcast.2.block_ref, bf16[128,1536]{1,0:T(8,128)(2,1)S(1)} %collective-permute-done.13.refs_0_, bf16[128,2048]{1,0:T(8,128)(2,1)S(1)} %get-tuple-element.63.refs_0_.refs_1_, ...), custom_call_target="tpu_custom_call", output_to_operand_aliasing={{1}: (6, {})} | custom-call | flops 4831838208 | bytes 37748736 | tf_op jit(solution)/shard_map/down_gradient/pallas_call | solution.py:272
  107.5 0.3 collective-permute-start.19
  107.8 7.1 %up_gradient.6 = (f32[2048,128]{1,0:T(8,128)S(1)}, bf16[2048,6144]{1,0:T(8,128)(2,1)}, f32[1,6144]{1,0:T(1,128)S(1)}) custom-call(s32[1]{0:T(128)} %bitcast.2.block_ref, bf16[128,1536]{1,0:T(8,128)(2,1)S(1)} %collective-permute-done.16.refs_0_, bf16[2048,128]{1,0:T(8,128)(2,1)S(1)} %get-tuple-element.69.refs_1_, ...), custom_call_target="tpu_custom_call", output_to_operand_aliasing={{1}: (6, {})} | custom-call | flops 4831838208 | bytes 37748736 | tf_op jit(solution)/shard_map/up_gradient/pallas_call | solution.py:272
  114.9 0.0 copy-start.1
  114.9 4.0 %down_gradient.7 = (f32[64,2048]{1,0:T(8,128)S(1)}, bf16[64,2048]{1,0:T(8,128)(2,1)S(1)}, bf16[6144,2048]{1,0:T(8,128)(2,1)}) custom-call(s32[1]{0:T(128)} %bitcast.block_ref, bf16[128,1536]{1,0:T(8,128)(2,1)S(1)} %collective-permute-done.15.refs_0_, bf16[128,2048]{1,0:T(8,128)(2,1)S(1)} %get-tuple-element.63.refs_0_.refs_1_, ...), custom_call_target="tpu_custom_call", output_to_operand_aliasing={{2}: (5, {})} | custom-call | flops 4831838208 | bytes 37748736 | tf_op jit(solution)/shard_map/down_gradient/pallas_call | solution.py:272
  118.9 0.1 collective-permute-start.17
  119.1 1.9 %last_product.1 = (f32[64,2048]{1,0:T(8,128)S(1)}, bf16[64,2048]{1,0:T(8,128)(2,1)S(1)}) custom-call(bf16[128,1536]{1,0:T(8,128)(2,1)S(1)} %collective-permute-done.19.act_ref.refs_0_, bf16[2048,1536]{1,0:T(8,128)(2,1)S(1)} %get-tuple-element.92.weights_ref, f32[2048,128]{1,0:T(8,128)S(1)} %get-tuple-element.88.refs_5_.total_in, ...), custom_call_target="tpu_custom_call" | custom-call | flops 2415919104 | bytes 18874368 | tf_op jit(solution)/shard_map/last_product/pallas_call | solution.py:411
  121.0 0.5 collective-permute-start.20
  121.6 1.3 %collective-permute-start.18 = (bf16[32,2048]{1,0:T(8,128)(2,1)S(1)}, bf16[32,2048]{1,0:T(8,128)(2,1)S(1)}, u32[]{:S(2)}, u32[]{:S(2)}) collective-permute-start(bf16[32,2048]{1,0:T(8,128)(2,1)S(1)} %slice.33), channel_id=1, source_target_pairs={{0,8},{4,12},{8,0},{12,4},{1,9},{5,13},{9,1},{13,5},{2,10},{6,14},... | collective-permute-start | bytes 393224 | tf_op jit(solution)/shard_map/ppermute | solution.py:446
  122.9 0.1 convert_add_fusion
  123.0 1.1 collective-permute-start.21
  124.1 4.2 %up_gradient.7 = (bf16[2048,6144]{1,0:T(8,128)(2,1)}, f32[1,6144]{1,0:T(1,128)}) custom-call(s32[1]{0:T(128)} %bitcast.block_ref, bf16[128,1536]{1,0:T(8,128)(2,1)S(1)} %collective-permute-done.19.act_ref.refs_0_, bf16[2048,128]{1,0:T(8,128)(2,1)S(1)} %get-tuple-element.69.refs_1_, ...), custom_call_target="tpu_custom_call", output_to_operand_aliasing={{0}: (3, {})} | custom-call | flops 4831838208 | bytes 18874368 | tf_op jit(solution)/shard_map/up_gradient/pallas_call | solution.py:272
  128.4 0.7 fusion.2
  129.1 0.9 collective-permute-done.21
  129.9 0.7 fusion
  (17 shorter events, 0.1 us)
Async XLA Ops:
  0.6 13.9 %copy-start = (bf16[32,2048]{1,0:T(8,128)(2,1)S(1)}, bf16[32,2048]{1,0:T(8,128)(2,1)}, u32[]{:S(2)}) copy-start(bf16[32,2048]{1,0:T(8,128)(2,1)} %refs_0_.2) | copy-start | bytes 393220
  0.6 6.7 %collective-permute-start = (bf16[32,2048]{1,0:T(8,128)(2,1)}, bf16[32,2048]{1,0:T(8,128)(2,1)S(1)}, u32[]{:S(2)}, u32[]{:S(2)}) collective-permute-start(bf16[32,2048]{1,0:T(8,128)(2,1)} %refs_0_.1), channel_id=1, source_target_pairs={{0,8},{4,12},{8,0},{12,4},{1,9},{5,13},{9,1},{13,5},{2,10},{6,14},... | collective-permute-start | bytes 393224 | tf_op jit(solution)/shard_map/ppermute | solution.py:436
  3.7 5.5 %collective-permute-start.1 = (bf16[32,2048]{1,0:T(8,128)(2,1)}, bf16[32,2048]{1,0:T(8,128)(2,1)S(1)}, u32[]{:S(2)}, u32[]{:S(2)}) collective-permute-start(bf16[32,2048]{1,0:T(8,128)(2,1)} %refs_0_.1), channel_id=1, source_target_pairs={{0,4},{4,0},{8,12},{12,8},{1,5},{5,1},{9,13},{13,9},{2,6},{6,2},{1... | collective-permute-start | bytes 393224 | tf_op jit(solution)/shard_map/ppermute | solution.py:441
  7.4 1.7 %collective-permute-start.2 = (bf16[32,2048]{1,0:T(8,128)(2,1)S(1)}, bf16[32,2048]{1,0:T(8,128)(2,1)S(1)}, u32[]{:S(2)}, u32[]{:S(2)}) collective-permute-start(bf16[32,2048]{1,0:T(8,128)(2,1)S(1)} %collective-permute-done.refs_1_), channel_id=1, source_target_pairs={{0,4},{4,0},{8,12},{12,8},{1,5},{5,1},{9,13},{13,9},{2,6},{6,2},{1... | collective-permute-start | bytes 393224 | tf_op jit(solution)/shard_map/ppermute | solution.py:441
  7.4 7.1 %collective-permute-start.7 = (bf16[32,2048]{1,0:T(8,128)(2,1)}, bf16[32,2048]{1,0:T(8,128)(2,1)S(1)}, u32[]{:S(2)}, u32[]{:S(2)}) collective-permute-start(bf16[32,2048]{1,0:T(8,128)(2,1)} %refs_0_.2), channel_id=1, source_target_pairs={{0,8},{4,12},{8,0},{12,4},{1,9},{5,13},{9,1},{13,5},{2,10},{6,14},... | collective-permute-start | bytes 393224 | tf_op jit(solution)/shard_map/ppermute | solution.py:436
  12.9 13.8 %collective-permute-start.3 = (bf16[128,1536]{1,0:T(8,128)(2,1)S(1)}, bf16[128,1536]{1,0:T(8,128)(2,1)S(1)}, u32[]{:S(2)}, u32[]{:S(2)}) collective-permute-start(bf16[128,1536]{1,0:T(8,128)(2,1)S(1)} %get-tuple-element.55), channel_id=1, source_target_pairs={{0,1},{1,2},{2,3},{3,0},{4,5},{5,6},{6,7},{7,4},{8,9},{9,10},{10,1... | collective-permute-start | bytes 1179656 | tf_op jit(solution)/shard_map/ppermute | solution.py:453
  14.5 1.3 %collective-permute-start.8 = (bf16[32,2048]{1,0:T(8,128)(2,1)S(1)}, bf16[32,2048]{1,0:T(8,128)(2,1)S(1)}, u32[]{:S(2)}, u32[]{:S(2)}) collective-permute-start(bf16[32,2048]{1,0:T(8,128)(2,1)S(1)} %copy-done), channel_id=1, source_target_pairs={{0,4},{4,0},{8,12},{12,8},{1,5},{5,1},{9,13},{13,9},{2,6},{6,2},{1... | collective-permute-start | bytes 393224 | tf_op jit(solution)/shard_map/ppermute | solution.py:441
  14.5 1.5 %collective-permute-start.9 = (bf16[32,2048]{1,0:T(8,128)(2,1)S(1)}, bf16[32,2048]{1,0:T(8,128)(2,1)S(1)}, u32[]{:S(2)}, u32[]{:S(2)}) collective-permute-start(bf16[32,2048]{1,0:T(8,128)(2,1)S(1)} %collective-permute-done.7.refs_1_), channel_id=1, source_target_pairs={{0,4},{4,0},{8,12},{12,8},{1,5},{5,1},{9,13},{13,9},{2,6},{6,2},{1... | collective-permute-start | bytes 393224 | tf_op jit(solution)/shard_map/ppermute | solution.py:441
  20.5 14.6 %collective-permute-start.10 = (bf16[128,1536]{1,0:T(8,128)(2,1)S(1)}, bf16[128,1536]{1,0:T(8,128)(2,1)S(1)}, u32[]{:S(2)}, u32[]{:S(2)}) collective-permute-start(bf16[128,1536]{1,0:T(8,128)(2,1)S(1)} %get-tuple-element.64), channel_id=1, source_target_pairs={{0,1},{1,2},{2,3},{3,0},{4,5},{5,6},{6,7},{7,4},{8,9},{9,10},{10,1... | collective-permute-start | bytes 1179656 | tf_op jit(solution)/shard_map/ppermute | solution.py:453
  30.5 12.4 %collective-permute-start.4 = (bf16[128,1536]{1,0:T(8,128)(2,1)S(1)}, bf16[128,1536]{1,0:T(8,128)(2,1)S(1)}, u32[]{:S(2)}, u32[]{:S(2)}) collective-permute-start(bf16[128,1536]{1,0:T(8,128)(2,1)S(1)} %up_share.5), channel_id=1, source_target_pairs={{0,1},{1,2},{2,3},{3,0},{4,5},{5,6},{6,7},{7,4},{8,9},{9,10},{10,1... | collective-permute-start | bytes 1179656 | tf_op jit(solution)/shard_map/ppermute | solution.py:453
  39.6 13.3 %collective-permute-start.11 = (bf16[128,1536]{1,0:T(8,128)(2,1)S(1)}, bf16[128,1536]{1,0:T(8,128)(2,1)S(1)}, u32[]{:S(2)}, u32[]{:S(2)}) collective-permute-start(bf16[128,1536]{1,0:T(8,128)(2,1)S(1)} %down_share.5), channel_id=1, source_target_pairs={{0,1},{1,2},{2,3},{3,0},{4,5},{5,6},{6,7},{7,4},{8,9},{9,10},{10,1... | collective-permute-start | bytes 1179656 | tf_op jit(solution)/shard_map/ppermute | solution.py:453
  46.7 14.4 %collective-permute-start.5 = (bf16[128,1536]{1,0:T(8,128)(2,1)S(1)}, bf16[128,1536]{1,0:T(8,128)(2,1)S(1)}, u32[]{:S(2)}, u32[]{:S(2)}) collective-permute-start(bf16[128,1536]{1,0:T(8,128)(2,1)S(1)} %get-tuple-element.56), channel_id=1, source_target_pairs={{0,1},{1,2},{2,3},{3,0},{4,5},{5,6},{6,7},{7,4},{8,9},{9,10},{10,1... | collective-permute-start | bytes 1179656 | tf_op jit(solution)/shard_map/ppermute | solution.py:453
  57.5 13.9 %collective-permute-start.12 = (bf16[128,1536]{1,0:T(8,128)(2,1)S(1)}, bf16[128,1536]{1,0:T(8,128)(2,1)S(1)}, u32[]{:S(2)}, u32[]{:S(2)}) collective-permute-start(bf16[128,1536]{1,0:T(8,128)(2,1)S(1)} %get-tuple-element.65), channel_id=1, source_target_pairs={{0,1},{1,2},{2,3},{3,0},{4,5},{5,6},{6,7},{7,4},{8,9},{9,10},{10,1... | collective-permute-start | bytes 1179656 | tf_op jit(solution)/shard_map/ppermute | solution.py:453
  61.8 18.8 %collective-permute-start.6 = (bf16[128,1536]{1,0:T(8,128)(2,1)S(1)}, bf16[128,1536]{1,0:T(8,128)(2,1)S(1)}, u32[]{:S(2)}, u32[]{:S(2)}) collective-permute-start(bf16[128,1536]{1,0:T(8,128)(2,1)S(1)} %get-tuple-element.59.refs_0_), channel_id=1, source_target_pairs={{0,1},{1,2},{2,3},{3,0},{4,5},{5,6},{6,7},{7,4},{8,9},{9,10},{10,1... | collective-permute-start | bytes 1179656 | tf_op jit(solution)/shard_map/ppermute | solution.py:453
  71.5 16.7 %collective-permute-start.14 = (bf16[128,1536]{1,0:T(8,128)(2,1)S(1)}, bf16[128,1536]{1,0:T(8,128)(2,1)S(1)}, u32[]{:S(2)}, u32[]{:S(2)}) collective-permute-start(bf16[128,1536]{1,0:T(8,128)(2,1)S(1)} %multiply_convert_fusion.refs_3_.refs_0_), channel_id=1, source_target_pairs={{0,1},{1,2},{2,3},{3,0},{4,5},{5,6},{6,7},{7,4},{8,9},{9,10},{10,1... | collective-permute-start | bytes 1179656 | tf_op jit(solution)/shard_map/ppermute | solution.py:453
  80.6 16.1 %collective-permute-start.13 = (bf16[128,1536]{1,0:T(8,128)(2,1)S(1)}, bf16[128,1536]{1,0:T(8,128)(2,1)S(1)}, u32[]{:S(2)}, u32[]{:S(2)}) collective-permute-start(bf16[128,1536]{1,0:T(8,128)(2,1)S(1)} %collective-permute-done.6.refs_0_), channel_id=1, source_target_pairs={{0,1},{1,2},{2,3},{3,0},{4,5},{5,6},{6,7},{7,4},{8,9},{9,10},{10,1... | collective-permute-start | bytes 1179656 | tf_op jit(solution)/shard_map/ppermute | solution.py:453
  88.2 19.2 %collective-permute-start.16 = (bf16[128,1536]{1,0:T(8,128)(2,1)S(1)}, bf16[128,1536]{1,0:T(8,128)(2,1)S(1)}, u32[]{:S(2)}, u32[]{:S(2)}) collective-permute-start(bf16[128,1536]{1,0:T(8,128)(2,1)S(1)} %collective-permute-done.14.refs_0_), channel_id=1, source_target_pairs={{0,1},{1,2},{2,3},{3,0},{4,5},{5,6},{6,7},{7,4},{8,9},{9,10},{10,1... | collective-permute-start | bytes 1179656 | tf_op jit(solution)/shard_map/ppermute | solution.py:453
  96.7 18.2 %collective-permute-start.15 = (bf16[128,1536]{1,0:T(8,128)(2,1)S(1)}, bf16[128,1536]{1,0:T(8,128)(2,1)S(1)}, u32[]{:S(2)}, u32[]{:S(2)}) collective-permute-start(bf16[128,1536]{1,0:T(8,128)(2,1)S(1)} %collective-permute-done.13.refs_0_), channel_id=1, source_target_pairs={{0,1},{1,2},{2,3},{3,0},{4,5},{5,6},{6,7},{7,4},{8,9},{9,10},{10,1... | collective-permute-start | bytes 1179656 | tf_op jit(solution)/shard_map/ppermute | solution.py:453
  107.5 11.6 %collective-permute-start.19 = (bf16[128,1536]{1,0:T(8,128)(2,1)S(1)}, bf16[128,1536]{1,0:T(8,128)(2,1)S(1)}, u32[]{:S(2)}, u32[]{:S(2)}) collective-permute-start(bf16[128,1536]{1,0:T(8,128)(2,1)S(1)} %collective-permute-done.16.refs_0_), channel_id=1, source_target_pairs={{0,1},{1,2},{2,3},{3,0},{4,5},{5,6},{6,7},{7,4},{8,9},{9,10},{10,1... | collective-permute-start | bytes 1179656 | tf_op jit(solution)/shard_map/ppermute | solution.py:453
  114.9 4.1 %copy-start.1 = (bf16[2048]{0:T(1024)(128)(2,1)S(1)}, bf16[2048]{0:T(1024)(128)(2,1)}, u32[]{:S(2)}) copy-start(bf16[2048]{0:T(1024)(128)(2,1)} %param.14) | copy-start | bytes 12292
  118.9 2.6 %collective-permute-start.17 = (bf16[64,2048]{1,0:T(8,128)(2,1)S(1)}, bf16[64,2048]{1,0:T(8,128)(2,1)S(1)}, u32[]{:S(2)}, u32[]{:S(2)}) collective-permute-start(bf16[64,2048]{1,0:T(8,128)(2,1)S(1)} %get-tuple-element.90.after_ref), channel_id=1, source_target_pairs={{0,4},{4,0},{8,12},{12,8},{1,5},{5,1},{9,13},{13,9},{2,6},{6,2},{1... | collective-permute-start | bytes 786440 | tf_op jit(solution)/shard_map/ppermute | solution.py:446
  121.0 2.0 %collective-permute-start.20 = (bf16[64,2048]{1,0:T(8,128)(2,1)S(1)}, bf16[64,2048]{1,0:T(8,128)(2,1)S(1)}, u32[]{:S(2)}, u32[]{:S(2)}) collective-permute-start(bf16[64,2048]{1,0:T(8,128)(2,1)S(1)} %get-tuple-element.94), channel_id=1, source_target_pairs={{0,4},{4,0},{8,12},{12,8},{1,5},{5,1},{9,13},{13,9},{2,6},{6,2},{1... | collective-permute-start | bytes 786440 | tf_op jit(solution)/shard_map/ppermute | solution.py:446
  121.6 6.8 %collective-permute-start.18 = (bf16[32,2048]{1,0:T(8,128)(2,1)S(1)}, bf16[32,2048]{1,0:T(8,128)(2,1)S(1)}, u32[]{:S(2)}, u32[]{:S(2)}) collective-permute-start(bf16[32,2048]{1,0:T(8,128)(2,1)S(1)} %slice.33), channel_id=1, source_target_pairs={{0,8},{4,12},{8,0},{12,4},{1,9},{5,13},{9,1},{13,5},{2,10},{6,14},... | collective-permute-start | bytes 393224 | tf_op jit(solution)/shard_map/ppermute | solution.py:446
  123.0 6.9 %collective-permute-start.21 = (bf16[32,2048]{1,0:T(8,128)(2,1)S(1)}, bf16[32,2048]{1,0:T(8,128)(2,1)S(1)}, u32[]{:S(2)}, u32[]{:S(2)}) collective-permute-start(bf16[32,2048]{1,0:T(8,128)(2,1)S(1)} %slice.32.refs_4_), channel_id=1, source_target_pairs={{0,8},{4,12},{8,0},{12,4},{1,9},{5,13},{9,1},{13,5},{2,10},{6,14},... | collective-permute-start | bytes 393224 | tf_op jit(solution)/shard_map/ppermute | solution.py:446
where the time goes:
time: 131 us
  Pallas kernels  81.4 us (62%)
  waiting for transfers between devices  27 us (21%)
  starting transfers between devices  16.8 us (13%)
  local copies, waits for them, and re-layouts  2.78 us (2%)
  other arithmetic  1.62 us (1%)
    pallas_call x16, Pallas kernels, call(): pl.pallas_call(kernel, in_specs=operands.specs, out_specs=[spec for _, sp...  78.8 us
    ppermute x12, waiting for transfers between devices, passed_on(): return lax.ppermute(block, 'mp', ring)  24.2 us
    ppermute x12, starting transfers between devices, passed_on(): return lax.ppermute(block, 'mp', ring)  8.46 us
    ppermute x2, starting transfers between devices, first_exchange(): return [own_rows, lax.ppermute(own_rows, 'hidden', partner_pairs(bits[0]))]  4.77 us
    ppermute x4, starting transfers between devices, scattered_sum(): lax.ppermute(sent, 'hidden', partner_pairs(bit)).astype(jnp.float32)  3.04 us
  transfers between devices with their start and end apart: 22, of which 12 were waited for; matrix products, arithmetic and copies ran while one was open for 3% of the time, Pallas kernels for 62%

commit v1 on v0

--- a/solution.py
+++ b/solution.py
@@ -11,7 +11,8 @@
 cubic_coef = 0.044715
 LANES = 128
 MIB = 1024 * 1024
-COST_SCALE = 3
+SHARE_COST = 3
+GRADIENT_COST = 3
 SHARE_MIB = 4
 GRADIENT_MIB = 12
 DOWN_UNROLL = 3
@@ -218,6 +219,10 @@
     def work(index):
         columns = span(index * piece, piece)
         act = block_act[:, columns]
+        if summed and not kept_weights:
+            copy(index).wait()
+            scaled = up_scaled if up else down_scaled
+            scaled(side, weights_ref, scales_ref, block, index * piece, piece)
         if up:
             gradient = plain_product(rows_ref[...], act)
             bias_ref[0:1, span(block * block_width + index * piece, piece)] = jnp.sum(
@@ -226,17 +231,11 @@
         else:
             gradient = transposed_product(act, rows_ref[...])
         staged[index] = gradient.astype(jnp.bfloat16)
+        if summed and up:
+            total_ref[...] += product_transposed(weights_ref[:, columns], act)
+        elif summed:
+            total_ref[...] += plain_product(act, weights_ref[columns, :])
         write(index).start()
-        if not summed:
-            return
-        if not kept_weights:
-            copy(index).wait()
-            scaled = up_scaled if up else down_scaled
-            scaled(side, weights_ref, scales_ref, block, index * piece, piece)
-        if up:
-            total_ref[...] += product_transposed(weights_ref[:, columns], act)
-        else:
-            total_ref[...] += plain_product(act, weights_ref[columns, :])
 
     each(count, work, GRADIENT_UNROLL)
     if last and summed:
@@ -246,10 +245,10 @@
     each(count, lambda index: write(index).wait())
 
 
-def cost_of(token_count, width, hidden_count, products, passes):
+def cost_of(scale, token_count, width, hidden_count, products, passes):
     return pl.CostEstimate(
-        flops=COST_SCALE * 2 * products * token_count * width * hidden_count,
-        bytes_accessed=COST_SCALE * 2 * passes * width * hidden_count,
+        flops=int(scale * 2 * products * token_count * width * hidden_count),
+        bytes_accessed=int(scale * 2 * passes * width * hidden_count),
         transcendentals=0,
     )
 
@@ -325,7 +324,7 @@
         ([] if keep else [weights])
         + [pltpu.SemaphoreType.DMA((sizes.block_width // piece + 1,))]
         + ([] if sum_in is None else [pltpu.VMEM((sizes.rows, sizes.block_width), jnp.bfloat16)]),
-        cost_of(sizes.rows, sizes.width, sizes.block_width, 1, 1),
+        cost_of(SHARE_COST, sizes.rows, sizes.width, sizes.block_width, 1, 1),
         SHARE_MIB if keep else SHARE_MIB + 7,
     )
 
@@ -385,7 +384,7 @@
         operands,
         outs,
         scratch,
-        cost_of(sizes.rows, sizes.width, sizes.block_width, 2, 2 if summed else 1),
+        cost_of(GRADIENT_COST, sizes.rows, sizes.width, sizes.block_width, 2, 2 if summed else 1),
         GRADIENT_MIB if kept else GRADIENT_MIB + 7,
         aliases,
     )
@@ -416,14 +415,15 @@
             jax.ShapeDtypeStruct(half_shape, jnp.float32),
             jax.ShapeDtypeStruct(half_shape, jnp.bfloat16),
         ],
-        cost_estimate=cost_of(sizes.rows, sizes.width, sizes.block_width, 1, 1),
+        cost_estimate=cost_of(SHARE_COST, sizes.rows, sizes.width, sizes.block_width, 1, 1),
         name="last_product",
         compiler_params=pltpu.CompilerParams(vmem_limit_bytes=SHARE_MIB * MIB),
     )(block_act, pltpu.with_memory_space_constraint(weights, pltpu.VMEM), total_in, after)
 
 
 def ring_program(mp_count, hidden_count):
-    ring = [(i, (i + 1) % mp_count) for i in range(mp_count)]
+    order = [0, *range(1, mp_count, 2), *reversed(range(2, mp_count, 2))]
+    ring = [(order[i], order[(i + 1) % mp_count]) for i in range(mp_count)]
     bits = [1 << bit for bit in reversed(range(hidden_count.bit_length() - 1))]
 
     def partner_pairs(bit):
@@ -462,15 +462,16 @@
         side = width // up_scales.shape[0]
         block_width = hidden // mp_count
         sizes = Sizes(tokens.shape[0] * hidden_count, width, hidden, block_width, side)
-        me = lax.axis_index("mp").astype(jnp.int32)
+        index = lax.axis_index("mp").astype(jnp.int32)
+        me = jnp.where(index % 2 == 1, (index + 1) // 2, (mp_count - index // 2) % mp_count)
 
         up_wide = jnp.repeat(up_scales, side, axis=1)
         down_wide = jnp.repeat(down_scales, side, axis=1).reshape(mp_count, -1, width)
-        token_rows = first_exchange(tokens)
-        cot_rows = first_exchange(after(cotangent, token_rows[1]))
         own_bias = lax.dynamic_slice(
             up_bias.reshape(1, hidden), (0, me * block_width), (1, block_width)
         )
+        token_rows = first_exchange(tokens)
+        cot_rows = first_exchange(after(cotangent, up_wide, down_wide, own_bias))
         token_rows = later_exchanges(token_rows, up_wide, down_wide, own_bias)
 
         def block_number(back):
@@ -519,15 +520,15 @@
         output_held = input_held = None
         for back in range(mp_count):
             last = back == mp_count - 1
-            sent_act = act_block if back == 0 else after(act_block, input_held[0])
+            sent_act = act_block if back == 0 else after(act_block, output_held[0])
             next_act = None if last else passed_on(sent_act)
+            sent_pre = pre_block if back == 0 else after(pre_block, input_held[0])
+            next_pre = None if last else passed_on(sent_pre)
             output_held = gradient_call(
                 sizes, False, block_number(back), act_block, cot_rows, down_weights.get(back),
                 down_codes, down_wide, output_held,
                 pre_block if back == 0 else input_held[0], last,
             )
-            sent_pre = pre_block if back == 0 else after(pre_block, output_held[0])
-            next_pre = None if last else passed_on(sent_pre)
             if last:
                 output_sum, output_sent = scattered_sum(output_held[0], output_held[1])
                 tokens_kept, tokens_sent = product_call(

time: 131 us -> 130 us (level)
  waiting for transfers between devices: 27 us -> 16.8 us
  starting transfers between devices: 16.8 us -> 26.9 us
    ppermute x12, waiting for transfers between devices: 24.2 us -> 13.9 us  [passed_on(): return lax.ppermute(block, 'mp', ring)]
    ppermute x12, starting transfers between devices: 8.46 us -> 18.7 us  [passed_on(): return lax.ppermute(block, 'mp', ring)]
  transfers between devices with their start and end apart: 22 -> 22, of which waited for: 12 -> 11; matrix products, arithmetic and copies ran while one was open for 3% -> 3% of each run, Pallas kernels for 62% -> 62%
where the time goes in v1:
time: 130 us; the launch traced here: 129 us
  Pallas kernels  80.3 us (62%)
  starting transfers between devices  26.9 us (21%)
  waiting for transfers between devices  16.8 us (13%)
  local copies, waits for them, and re-layouts  2.78 us (2%)
  other arithmetic  1.62 us (1%)
    pallas_call x16, Pallas kernels, call(): pl.pallas_call(kernel, in_specs=operands.specs, out_specs=[spec for _, sp...  77.7 us
    ppermute x12, starting transfers between devices, passed_on(): return lax.ppermute(block, 'mp', ring)  18.7 us
    ppermute x12, waiting for transfers between devices, passed_on(): return lax.ppermute(block, 'mp', ring)  13.9 us
    ppermute x2, starting transfers between devices, first_exchange(): return [own_rows, lax.ppermute(own_rows, 'hidden', partner_pairs(bits[0]))]  4.77 us
    ppermute x4, starting transfers between devices, scattered_sum(): lax.ppermute(sent, 'hidden', partner_pairs(bit)).astype(jnp.float32)  2.92 us
  transfers between devices with their start and end apart: 22, of which 11 were waited for; matrix products, arithmetic and copies ran while one was open for 3% of the time, Pallas kernels for 62%

profile of v1, /device:TPU:0, one launch (start us, length us, event | category | flops | bytes accessed | tf_op | source)
XLA Modules:
  0.0 129.3 jit_solution(10407227421260430351)
XLA Ops:
  0.6 0.0 copy-start
  0.6 3.0 %collective-permute-start = (bf16[32,2048]{1,0:T(8,128)(2,1)}, bf16[32,2048]{1,0:T(8,128)(2,1)S(1)}, u32[]{:S(2)}, u32[]{:S(2)}) collective-permute-start(bf16[32,2048]{1,0:T(8,128)(2,1)} %refs_0_.1), channel_id=1, source_target_pairs={{0,8},{4,12},{8,0},{12,4},{1,9},{5,13},{9,1},{13,5},{2,10},{6,14},... | collective-permute-start | bytes 393224 | tf_op jit(solution)/shard_map/ppermute | solution.py:436
  3.7 0.0 collective-permute-start.1
  3.7 0.8 dynamic-slice.3
  4.5 0.8 copy.20
  5.2 0.2 broadcast_in_dim.8
  5.4 0.1 reshape_reshape.3.refs_5_.refs_2_.refs_3_
  5.5 0.9 broadcast_in_dim.7
  6.3 0.1 copy.23
  6.5 0.9 collective-permute-done.refs_1_
  7.4 1.7 %collective-permute-start.7 = (bf16[32,2048]{1,0:T(8,128)(2,1)}, bf16[32,2048]{1,0:T(8,128)(2,1)S(1)}, u32[]{:S(2)}, u32[]{:S(2)}) collective-permute-start(bf16[32,2048]{1,0:T(8,128)(2,1)} %refs_0_.2), channel_id=1, source_target_pairs={{0,8},{4,12},{8,0},{12,4},{1,9},{5,13},{9,1},{13,5},{2,10},{6,14},... | collective-permute-start | bytes 393224 | tf_op jit(solution)/shard_map/ppermute | solution.py:436
  9.1 0.0 collective-permute-done.1.refs_2_
  9.1 0.0 collective-permute-done.2.refs_3_
  9.1 3.7 %up_share.4 = (bf16[128,1536]{1,0:T(8,128)(2,1)S(1)}, bf16[128,2048]{1,0:T(8,128)(2,1)S(1)}) custom-call(s32[1]{0:T(128)} %bitcast.1.block_ref, bf16[32,2048]{1,0:T(8,128)(2,1)} %refs_0_.1, bf16[32,2048]{1,0:T(8,128)(2,1)S(1)} %collective-permute-done.refs_1_, bf16[32,2048]{1,0:T(8,128)(2,1)S(1)} %collective-permute-done.1.refs_2_, ...), custom_call_target="tpu_custom_call" | custom-call | flops 2415919104 | bytes 18874368 | tf_op jit(solution)/shard_map/up_share/pallas_call | solution.py:271
  12.9 1.6 %collective-permute-start.3 = (bf16[128,1536]{1,0:T(8,128)(2,1)S(1)}, bf16[128,1536]{1,0:T(8,128)(2,1)S(1)}, u32[]{:S(2)}, u32[]{:S(2)}) collective-permute-start(bf16[128,1536]{1,0:T(8,128)(2,1)S(1)} %get-tuple-element.55), channel_id=1, source_target_pairs={{0,1},{1,3},{3,2},{2,0},{4,5},{5,7},{7,6},{6,4},{8,9},{9,11},{11,1... | collective-permute-start | bytes 1179656 | tf_op jit(solution)/shard_map/ppermute | solution.py:453
  14.5 0.0 collective-permute-done.7.refs_1_
  14.5 0.5 collective-permute-start.9
  15.0 0.8 collective-permute-done.8.refs_2_
  15.8 0.2 collective-permute-done.9.refs_3_
  16.0 4.4 %down_share.4 = (bf16[128,1536]{1,0:T(8,128)(2,1)S(1)}, bf16[128,2048]{1,0:T(8,128)(2,1)S(1)}) custom-call(s32[1]{0:T(128)} %bitcast.1.block_ref, bf16[32,2048]{1,0:T(8,128)(2,1)} %refs_0_.2, bf16[32,2048]{1,0:T(8,128)(2,1)S(1)} %collective-permute-done.7.refs_1_, bf16[32,2048]{1,0:T(8,128)(2,1)S(1)} %collective-permute-done.8.refs_2_, ...), custom_call_target="tpu_custom_call" | custom-call | flops 2415919104 | bytes 18874368 | tf_op jit(solution)/shard_map/down_share/pallas_call | solution.py:271
  20.5 2.6 %collective-permute-start.10 = (bf16[128,1536]{1,0:T(8,128)(2,1)S(1)}, bf16[128,1536]{1,0:T(8,128)(2,1)S(1)}, u32[]{:S(2)}, u32[]{:S(2)}) collective-permute-start(bf16[128,1536]{1,0:T(8,128)(2,1)S(1)} %get-tuple-element.66), channel_id=1, source_target_pairs={{0,1},{1,3},{3,2},{2,0},{4,5},{5,7},{7,6},{6,4},{8,9},{9,11},{11,1... | collective-permute-start | bytes 1179656 | tf_op jit(solution)/shard_map/ppermute | solution.py:453
  23.1 2.6 %collective-permute-done.3.refs_3_ = bf16[128,1536]{1,0:T(8,128)(2,1)S(1)} collective-permute-done((bf16[128,1536]{1,0:T(8,128)(2,1)S(1)}, bf16[128,1536]{1,0:T(8,128)(2,1)S(1)}, u32[]{:S(2)}, u32[]{:S(2)}) %collective-permute-start.3) | collective-permute-done | bytes 393248 | tf_op jit(solution)/shard_map/ppermute | solution.py:453
  25.7 3.8 %up_share.5 = bf16[128,1536]{1,0:T(8,128)(2,1)S(1)} custom-call(s32[1]{0:T(128)} %bitcast.2.block_ref, bf16[128,2048]{1,0:T(8,128)(2,1)S(1)} %get-tuple-element.54.refs_0_, bf16[2048,6144]{1,0:T(8,128)(2,1)} %refs_2_.7, f32[16,6144]{1,0:T(8,128)S(1)} %bitcast.10, bf16[128,1536]{1,0:T(8,128)(2,1)S(1)} %collective-permute-done.3.refs_3_), custom_call_target="tpu_custom_call" | custom-call | flops 2415919104 | bytes 18874368 | tf_op jit(solution)/shard_map/up_share/pallas_call | solution.py:271
  29.5 0.9 collective-permute-start.4
  30.4 3.7 %collective-permute-done.10.refs_3_ = bf16[128,1536]{1,0:T(8,128)(2,1)S(1)} collective-permute-done((bf16[128,1536]{1,0:T(8,128)(2,1)S(1)}, bf16[128,1536]{1,0:T(8,128)(2,1)S(1)}, u32[]{:S(2)}, u32[]{:S(2)}) %collective-permute-start.10) | collective-permute-done | bytes 393248 | tf_op jit(solution)/shard_map/ppermute | solution.py:453
  34.1 4.6 %down_share.6 = bf16[128,1536]{1,0:T(8,128)(2,1)S(1)} custom-call(s32[1]{0:T(128)} %bitcast.2.block_ref, bf16[128,2048]{1,0:T(8,128)(2,1)S(1)} %get-tuple-element.62.refs_0_.refs_1_, bf16[6144,2048]{1,0:T(8,128)(2,1)} %refs_2_.6, f32[4,12,2048]{2,1,0:T(8,128)S(1)} %reshape_reshape.3.refs_5_.refs_2_.refs_3_, bf16[128,1536]{1,0:T(8,128)(2,1)S(1)} %collective-permute-done.10.refs_3_), custom_call_target="tpu_custom_call" | custom-call | flops 2415919104 | bytes 18874368 | tf_op jit(solution)/shard_map/down_share/pallas_call | solution.py:271
  38.7 1.0 collective-permute-start.11
  39.7 2.9 %collective-permute-done.4.refs_3_ = bf16[128,1536]{1,0:T(8,128)(2,1)S(1)} collective-permute-done((bf16[128,1536]{1,0:T(8,128)(2,1)S(1)}, bf16[128,1536]{1,0:T(8,128)(2,1)S(1)}, u32[]{:S(2)}, u32[]{:S(2)}) %collective-permute-start.4) | collective-permute-done | bytes 393248 | tf_op jit(solution)/shard_map/ppermute | solution.py:453
  42.5 3.8 %up_share.6 = (bf16[128,1536]{1,0:T(8,128)(2,1)S(1)}, bf16[2048,128]{1,0:T(8,128)(2,1)S(1)}, bf16[2048,1536]{1,0:T(8,128)(2,1)S(1)}) custom-call(s32[1]{0:T(128)} %bitcast.block_ref, bf16[128,2048]{1,0:T(8,128)(2,1)S(1)} %get-tuple-element.54.refs_0_, bf16[2048,6144]{1,0:T(8,128)(2,1)} %refs_2_.7, f32[16,6144]{1,0:T(8,128)S(1)} %bitcast.11, ...), custom_call_target="tpu_custom_call" | custom-call | flops 2415919104 | bytes 18874368 | tf_op jit(solution)/shard_map/up_share/pallas_call | solution.py:271
  46.4 1.0 collective-permute-start.5
  47.4 3.6 %up_share.7 = (bf16[128,1536]{1,0:T(8,128)(2,1)S(1)}, bf16[2048,1536]{1,0:T(8,128)(2,1)S(1)}) custom-call(s32[1]{0:T(128)} %bitcast.3.block_ref, bf16[128,2048]{1,0:T(8,128)(2,1)S(1)} %get-tuple-element.54.refs_0_, bf16[2048,6144]{1,0:T(8,128)(2,1)} %refs_2_.7, f32[16,6144]{1,0:T(8,128)S(1)} %bitcast.12), custom_call_target="tpu_custom_call" | custom-call | flops 2415919104 | bytes 18874368 | tf_op jit(solution)/shard_map/up_share/pallas_call | solution.py:271
  51.0 0.7 collective-permute-done.11.refs_3_
  51.7 4.6 %down_share.7 = (bf16[128,1536]{1,0:T(8,128)(2,1)S(1)}, bf16[1536,2048]{1,0:T(8,128)(2,1)S(1)}) custom-call(s32[1]{0:T(128)} %bitcast.block_ref, bf16[128,2048]{1,0:T(8,128)(2,1)S(1)} %get-tuple-element.62.refs_0_.refs_1_, bf16[6144,2048]{1,0:T(8,128)(2,1)} %refs_2_.6, f32[4,12,2048]{2,1,0:T(8,128)S(1)} %reshape_reshape.3.refs_5_.refs_2_.refs_3_, ...), custom_call_target="tpu_custom_call" | custom-call | flops 2415919104 | bytes 18874368 | tf_op jit(solution)/shard_map/down_share/pallas_call | solution.py:271
  56.3 2.7 %collective-permute-start.12 = (bf16[128,1536]{1,0:T(8,128)(2,1)S(1)}, bf16[128,1536]{1,0:T(8,128)(2,1)S(1)}, u32[]{:S(2)}, u32[]{:S(2)}) collective-permute-start(bf16[128,1536]{1,0:T(8,128)(2,1)S(1)} %get-tuple-element.67), channel_id=1, source_target_pairs={{0,1},{1,3},{3,2},{2,0},{4,5},{5,7},{7,6},{6,4},{8,9},{9,11},{11,1... | collective-permute-start | bytes 1179656 | tf_op jit(solution)/shard_map/ppermute | solution.py:453
  59.0 0.6 collective-permute-done.5.sum_ref
  59.6 0.7 activation.1
  60.3 1.4 %collective-permute-start.6 = (bf16[128,1536]{1,0:T(8,128)(2,1)S(1)}, bf16[128,1536]{1,0:T(8,128)(2,1)S(1)}, u32[]{:S(2)}, u32[]{:S(2)}) collective-permute-start(bf16[128,1536]{1,0:T(8,128)(2,1)S(1)} %get-tuple-element.59.refs_0_), channel_id=1, source_target_pairs={{0,1},{1,3},{3,2},{2,0},{4,5},{5,7},{7,6},{6,4},{8,9},{9,11},{11,1... | collective-permute-start | bytes 1179656 | tf_op jit(solution)/shard_map/ppermute | solution.py:453
  61.7 4.3 %down_share.5 = (bf16[128,1536]{1,0:T(8,128)(2,1)S(1)}, bf16[1536,2048]{1,0:T(8,128)(2,1)S(1)}) custom-call(s32[1]{0:T(128)} %bitcast.3.block_ref, bf16[128,2048]{1,0:T(8,128)(2,1)S(1)} %get-tuple-element.62.refs_0_.refs_1_, bf16[6144,2048]{1,0:T(8,128)(2,1)} %refs_2_.6, f32[4,12,2048]{2,1,0:T(8,128)S(1)} %reshape_reshape.3.refs_5_.refs_2_.refs_3_), custom_call_target="tpu_custom_call" | custom-call | flops 2415919104 | bytes 18874368 | tf_op jit(solution)/shard_map/down_share/pallas_call | solution.py:271
  66.0 3.3 %collective-permute-done.12 = bf16[128,1536]{1,0:T(8,128)(2,1)S(1)} collective-permute-done((bf16[128,1536]{1,0:T(8,128)(2,1)S(1)}, bf16[128,1536]{1,0:T(8,128)(2,1)S(1)}, u32[]{:S(2)}, u32[]{:S(2)}) %collective-permute-start.12) | collective-permute-done | bytes 393248 | tf_op jit(solution)/shard_map/ppermute | solution.py:453
  69.3 0.1 multiply_convert_fusion.refs_3_.refs_0_
  69.4 2.0 %collective-permute-start.15 = (bf16[128,1536]{1,0:T(8,128)(2,1)S(1)}, bf16[128,1536]{1,0:T(8,128)(2,1)S(1)}, u32[]{:S(2)}, u32[]{:S(2)}) collective-permute-start(bf16[128,1536]{1,0:T(8,128)(2,1)S(1)} %multiply_convert_fusion.refs_3_.refs_0_), channel_id=1, source_target_pairs={{0,1},{1,3},{3,2},{2,0},{4,5},{5,7},{7,6},{6,4},{8,9},{9,11},{11,1... | collective-permute-start | bytes 1179656 | tf_op jit(solution)/shard_map/ppermute | solution.py:453
  71.4 4.0 %down_gradient.4 = (f32[128,2048]{1,0:T(8,128)S(1)}, bf16[6144,2048]{1,0:T(8,128)(2,1)}) custom-call(s32[1]{0:T(128)} %bitcast.3.block_ref, bf16[128,1536]{1,0:T(8,128)(2,1)S(1)} %get-tuple-element.59.refs_0_, bf16[128,2048]{1,0:T(8,128)(2,1)S(1)} %get-tuple-element.62.refs_0_.refs_1_, bf16[1536,2048]{1,0:T(8,128)(2,1)S(1)} %get-tuple-element.64.refs_2_, ...), custom_call_target="tpu_custom_call" | custom-call | flops 4831838208 | bytes 37748736 | tf_op jit(solution)/shard_map/down_gradient/pallas_call | solution.py:271
  75.4 4.8 %up_gradient.4 = (f32[2048,128]{1,0:T(8,128)S(1)}, bf16[2048,6144]{1,0:T(8,128)(2,1)}, f32[1,6144]{1,0:T(1,128)S(1)}) custom-call(s32[1]{0:T(128)} %bitcast.3.block_ref, bf16[128,1536]{1,0:T(8,128)(2,1)S(1)} %multiply_convert_fusion.refs_3_.refs_0_, bf16[2048,128]{1,0:T(8,128)(2,1)S(1)} %get-tuple-element.73.refs_1_, ...), custom_call_target="tpu_custom_call" | custom-call | flops 4831838208 | bytes 37748736 | tf_op jit(solution)/shard_map/up_gradient/pallas_call | solution.py:271
  80.2 2.5 %collective-permute-start.13 = (bf16[128,1536]{1,0:T(8,128)(2,1)S(1)}, bf16[128,1536]{1,0:T(8,128)(2,1)S(1)}, u32[]{:S(2)}, u32[]{:S(2)}) collective-permute-start(bf16[128,1536]{1,0:T(8,128)(2,1)S(1)} %collective-permute-done.6.refs_0_), channel_id=1, source_target_pairs={{0,1},{1,3},{3,2},{2,0},{4,5},{5,7},{7,6},{6,4},{8,9},{9,11},{11,1... | collective-permute-start | bytes 1179656 | tf_op jit(solution)/shard_map/ppermute | solution.py:453
  82.8 7.4 %down_gradient.5 = (f32[128,2048]{1,0:T(8,128)S(1)}, bf16[6144,2048]{1,0:T(8,128)(2,1)}) custom-call(s32[1]{0:T(128)} %bitcast.1.block_ref, bf16[128,1536]{1,0:T(8,128)(2,1)S(1)} %collective-permute-done.6.refs_0_, bf16[128,2048]{1,0:T(8,128)(2,1)S(1)} %get-tuple-element.62.refs_0_.refs_1_, ...), custom_call_target="tpu_custom_call", output_to_operand_aliasing={{1}: (6, {})} | custom-call | flops 4831838208 | bytes 37748736 | tf_op jit(solution)/shard_map/down_gradient/pallas_call | solution.py:271
  90.1 0.1 collective-permute-start.16
  90.2 6.5 %up_gradient.5 = (f32[2048,128]{1,0:T(8,128)S(1)}, bf16[2048,6144]{1,0:T(8,128)(2,1)}, f32[1,6144]{1,0:T(1,128)S(1)}) custom-call(s32[1]{0:T(128)} %bitcast.1.block_ref, bf16[128,1536]{1,0:T(8,128)(2,1)S(1)} %collective-permute-done.15.refs_0_, bf16[2048,128]{1,0:T(8,128)(2,1)S(1)} %get-tuple-element.73.refs_1_, ...), custom_call_target="tpu_custom_call", output_to_operand_aliasing={{1}: (6, {})} | custom-call | flops 4831838208 | bytes 37748736 | tf_op jit(solution)/shard_map/up_gradient/pallas_call | solution.py:271
  96.7 0.7 collective-permute-start.14
  97.5 7.4 %down_gradient.6 = (f32[128,2048]{1,0:T(8,128)S(1)}, bf16[6144,2048]{1,0:T(8,128)(2,1)}) custom-call(s32[1]{0:T(128)} %bitcast.2.block_ref, bf16[128,1536]{1,0:T(8,128)(2,1)S(1)} %collective-permute-done.13.refs_0_, bf16[128,2048]{1,0:T(8,128)(2,1)S(1)} %get-tuple-element.62.refs_0_.refs_1_, ...), custom_call_target="tpu_custom_call", output_to_operand_aliasing={{1}: (6, {})} | custom-call | flops 4831838208 | bytes 37748736 | tf_op jit(solution)/shard_map/down_gradient/pallas_call | solution.py:271
  104.8 2.0 %collective-permute-start.19 = (bf16[128,1536]{1,0:T(8,128)(2,1)S(1)}, bf16[128,1536]{1,0:T(8,128)(2,1)S(1)}, u32[]{:S(2)}, u32[]{:S(2)}) collective-permute-start(bf16[128,1536]{1,0:T(8,128)(2,1)S(1)} %collective-permute-done.16.refs_0_), channel_id=1, source_target_pairs={{0,1},{1,3},{3,2},{2,0},{4,5},{5,7},{7,6},{6,4},{8,9},{9,11},{11,1... | collective-permute-start | bytes 1179656 | tf_op jit(solution)/shard_map/ppermute | solution.py:453
  106.9 6.5 %up_gradient.6 = (f32[2048,128]{1,0:T(8,128)S(1)}, bf16[2048,6144]{1,0:T(8,128)(2,1)}, f32[1,6144]{1,0:T(1,128)S(1)}) custom-call(s32[1]{0:T(128)} %bitcast.2.block_ref, bf16[128,1536]{1,0:T(8,128)(2,1)S(1)} %collective-permute-done.16.refs_0_, bf16[2048,128]{1,0:T(8,128)(2,1)S(1)} %get-tuple-element.73.refs_1_, ...), custom_call_target="tpu_custom_call", output_to_operand_aliasing={{1}: (6, {})} | custom-call | flops 4831838208 | bytes 37748736 | tf_op jit(solution)/shard_map/up_gradient/pallas_call | solution.py:271
  113.4 0.0 copy-start.1
  113.4 4.0 %down_gradient.7 = (f32[64,2048]{1,0:T(8,128)S(1)}, bf16[64,2048]{1,0:T(8,128)(2,1)S(1)}, bf16[6144,2048]{1,0:T(8,128)(2,1)}) custom-call(s32[1]{0:T(128)} %bitcast.block_ref, bf16[128,1536]{1,0:T(8,128)(2,1)S(1)} %collective-permute-done.14.refs_0_, bf16[128,2048]{1,0:T(8,128)(2,1)S(1)} %get-tuple-element.62.refs_0_.refs_1_, ...), custom_call_target="tpu_custom_call", output_to_operand_aliasing={{2}: (5, {})} | custom-call | flops 4831838208 | bytes 37748736 | tf_op jit(solution)/shard_map/down_gradient/pallas_call | solution.py:271
  117.4 0.1 collective-permute-start.17
  117.5 0.2 collective-permute-done.19.act_ref.refs_0_
  117.7 1.9 %last_product.1 = (f32[64,2048]{1,0:T(8,128)S(1)}, bf16[64,2048]{1,0:T(8,128)(2,1)S(1)}) custom-call(bf16[128,1536]{1,0:T(8,128)(2,1)S(1)} %collective-permute-done.19.act_ref.refs_0_, bf16[2048,1536]{1,0:T(8,128)(2,1)S(1)} %get-tuple-element.92.weights_ref, f32[2048,128]{1,0:T(8,128)S(1)} %get-tuple-element.88.refs_5_.total_in, ...), custom_call_target="tpu_custom_call" | custom-call | flops 2415919104 | bytes 18874368 | tf_op jit(solution)/shard_map/last_product/pallas_call | solution.py:410
  119.7 0.3 collective-permute-start.20
  120.1 1.4 %collective-permute-start.18 = (bf16[32,2048]{1,0:T(8,128)(2,1)S(1)}, bf16[32,2048]{1,0:T(8,128)(2,1)S(1)}, u32[]{:S(2)}, u32[]{:S(2)}) collective-permute-start(bf16[32,2048]{1,0:T(8,128)(2,1)S(1)} %slice.33), channel_id=1, source_target_pairs={{0,8},{4,12},{8,0},{12,4},{1,9},{5,13},{9,1},{13,5},{2,10},{6,14},... | collective-permute-start | bytes 393224 | tf_op jit(solution)/shard_map/ppermute | solution.py:446
  121.5 0.1 convert_add_fusion
  121.6 1.1 collective-permute-start.21
  122.7 4.2 %up_gradient.7 = (bf16[2048,6144]{1,0:T(8,128)(2,1)}, f32[1,6144]{1,0:T(1,128)}) custom-call(s32[1]{0:T(128)} %bitcast.block_ref, bf16[128,1536]{1,0:T(8,128)(2,1)S(1)} %collective-permute-done.19.act_ref.refs_0_, bf16[2048,128]{1,0:T(8,128)(2,1)S(1)} %get-tuple-element.73.refs_1_, ...), custom_call_target="tpu_custom_call", output_to_operand_aliasing={{0}: (3, {})} | custom-call | flops 4831838208 | bytes 18874368 | tf_op jit(solution)/shard_map/up_gradient/pallas_call | solution.py:271
  126.9 0.7 fusion.2
  127.6 1.0 collective-permute-done.21
  128.6 0.7 fusion
  (17 shorter events, 0.1 us)
Async XLA Ops:
  0.6 13.9 %copy-start = (bf16[32,2048]{1,0:T(8,128)(2,1)S(1)}, bf16[32,2048]{1,0:T(8,128)(2,1)}, u32[]{:S(2)}) copy-start(bf16[32,2048]{1,0:T(8,128)(2,1)} %refs_0_.2) | copy-start | bytes 393220
  0.6 6.7 %collective-permute-start = (bf16[32,2048]{1,0:T(8,128)(2,1)}, bf16[32,2048]{1,0:T(8,128)(2,1)S(1)}, u32[]{:S(2)}, u32[]{:S(2)}) collective-permute-start(bf16[32,2048]{1,0:T(8,128)(2,1)} %refs_0_.1), channel_id=1, source_target_pairs={{0,8},{4,12},{8,0},{12,4},{1,9},{5,13},{9,1},{13,5},{2,10},{6,14},... | collective-permute-start | bytes 393224 | tf_op jit(solution)/shard_map/ppermute | solution.py:436
  3.7 5.5 %collective-permute-start.1 = (bf16[32,2048]{1,0:T(8,128)(2,1)}, bf16[32,2048]{1,0:T(8,128)(2,1)S(1)}, u32[]{:S(2)}, u32[]{:S(2)}) collective-permute-start(bf16[32,2048]{1,0:T(8,128)(2,1)} %refs_0_.1), channel_id=1, source_target_pairs={{0,4},{4,0},{8,12},{12,8},{1,5},{5,1},{9,13},{13,9},{2,6},{6,2},{1... | collective-permute-start | bytes 393224 | tf_op jit(solution)/shard_map/ppermute | solution.py:441
  7.4 1.7 %collective-permute-start.2 = (bf16[32,2048]{1,0:T(8,128)(2,1)S(1)}, bf16[32,2048]{1,0:T(8,128)(2,1)S(1)}, u32[]{:S(2)}, u32[]{:S(2)}) collective-permute-start(bf16[32,2048]{1,0:T(8,128)(2,1)S(1)} %collective-permute-done.refs_1_), channel_id=1, source_target_pairs={{0,4},{4,0},{8,12},{12,8},{1,5},{5,1},{9,13},{13,9},{2,6},{6,2},{1... | collective-permute-start | bytes 393224 | tf_op jit(solution)/shard_map/ppermute | solution.py:441
  7.4 7.1 %collective-permute-start.7 = (bf16[32,2048]{1,0:T(8,128)(2,1)}, bf16[32,2048]{1,0:T(8,128)(2,1)S(1)}, u32[]{:S(2)}, u32[]{:S(2)}) collective-permute-start(bf16[32,2048]{1,0:T(8,128)(2,1)} %refs_0_.2), channel_id=1, source_target_pairs={{0,8},{4,12},{8,0},{12,4},{1,9},{5,13},{9,1},{13,5},{2,10},{6,14},... | collective-permute-start | bytes 393224 | tf_op jit(solution)/shard_map/ppermute | solution.py:436
  12.9 12.8 %collective-permute-start.3 = (bf16[128,1536]{1,0:T(8,128)(2,1)S(1)}, bf16[128,1536]{1,0:T(8,128)(2,1)S(1)}, u32[]{:S(2)}, u32[]{:S(2)}) collective-permute-start(bf16[128,1536]{1,0:T(8,128)(2,1)S(1)} %get-tuple-element.55), channel_id=1, source_target_pairs={{0,1},{1,3},{3,2},{2,0},{4,5},{5,7},{7,6},{6,4},{8,9},{9,11},{11,1... | collective-permute-start | bytes 1179656 | tf_op jit(solution)/shard_map/ppermute | solution.py:453
  14.5 1.3 %collective-permute-start.8 = (bf16[32,2048]{1,0:T(8,128)(2,1)S(1)}, bf16[32,2048]{1,0:T(8,128)(2,1)S(1)}, u32[]{:S(2)}, u32[]{:S(2)}) collective-permute-start(bf16[32,2048]{1,0:T(8,128)(2,1)S(1)} %copy-done), channel_id=1, source_target_pairs={{0,4},{4,0},{8,12},{12,8},{1,5},{5,1},{9,13},{13,9},{2,6},{6,2},{1... | collective-permute-start | bytes 393224 | tf_op jit(solution)/shard_map/ppermute | solution.py:441
  14.5 1.5 %collective-permute-start.9 = (bf16[32,2048]{1,0:T(8,128)(2,1)S(1)}, bf16[32,2048]{1,0:T(8,128)(2,1)S(1)}, u32[]{:S(2)}, u32[]{:S(2)}) collective-permute-start(bf16[32,2048]{1,0:T(8,128)(2,1)S(1)} %collective-permute-done.7.refs_1_), channel_id=1, source_target_pairs={{0,4},{4,0},{8,12},{12,8},{1,5},{5,1},{9,13},{13,9},{2,6},{6,2},{1... | collective-permute-start | bytes 393224 | tf_op jit(solution)/shard_map/ppermute | solution.py:441
  20.5 13.6 %collective-permute-start.10 = (bf16[128,1536]{1,0:T(8,128)(2,1)S(1)}, bf16[128,1536]{1,0:T(8,128)(2,1)S(1)}, u32[]{:S(2)}, u32[]{:S(2)}) collective-permute-start(bf16[128,1536]{1,0:T(8,128)(2,1)S(1)} %get-tuple-element.66), channel_id=1, source_target_pairs={{0,1},{1,3},{3,2},{2,0},{4,5},{5,7},{7,6},{6,4},{8,9},{9,11},{11,1... | collective-permute-start | bytes 1179656 | tf_op jit(solution)/shard_map/ppermute | solution.py:453
  29.5 13.0 %collective-permute-start.4 = (bf16[128,1536]{1,0:T(8,128)(2,1)S(1)}, bf16[128,1536]{1,0:T(8,128)(2,1)S(1)}, u32[]{:S(2)}, u32[]{:S(2)}) collective-permute-start(bf16[128,1536]{1,0:T(8,128)(2,1)S(1)} %up_share.5), channel_id=1, source_target_pairs={{0,1},{1,3},{3,2},{2,0},{4,5},{5,7},{7,6},{6,4},{8,9},{9,11},{11,1... | collective-permute-start | bytes 1179656 | tf_op jit(solution)/shard_map/ppermute | solution.py:453
  38.7 13.0 %collective-permute-start.11 = (bf16[128,1536]{1,0:T(8,128)(2,1)S(1)}, bf16[128,1536]{1,0:T(8,128)(2,1)S(1)}, u32[]{:S(2)}, u32[]{:S(2)}) collective-permute-start(bf16[128,1536]{1,0:T(8,128)(2,1)S(1)} %down_share.6), channel_id=1, source_target_pairs={{0,1},{1,3},{3,2},{2,0},{4,5},{5,7},{7,6},{6,4},{8,9},{9,11},{11,1... | collective-permute-start | bytes 1179656 | tf_op jit(solution)/shard_map/ppermute | solution.py:453
  46.4 13.2 %collective-permute-start.5 = (bf16[128,1536]{1,0:T(8,128)(2,1)S(1)}, bf16[128,1536]{1,0:T(8,128)(2,1)S(1)}, u32[]{:S(2)}, u32[]{:S(2)}) collective-permute-start(bf16[128,1536]{1,0:T(8,128)(2,1)S(1)} %get-tuple-element.56), channel_id=1, source_target_pairs={{0,1},{1,3},{3,2},{2,0},{4,5},{5,7},{7,6},{6,4},{8,9},{9,11},{11,1... | collective-permute-start | bytes 1179656 | tf_op jit(solution)/shard_map/ppermute | solution.py:453
  56.3 13.0 %collective-permute-start.12 = (bf16[128,1536]{1,0:T(8,128)(2,1)S(1)}, bf16[128,1536]{1,0:T(8,128)(2,1)S(1)}, u32[]{:S(2)}, u32[]{:S(2)}) collective-permute-start(bf16[128,1536]{1,0:T(8,128)(2,1)S(1)} %get-tuple-element.67), channel_id=1, source_target_pairs={{0,1},{1,3},{3,2},{2,0},{4,5},{5,7},{7,6},{6,4},{8,9},{9,11},{11,1... | collective-permute-start | bytes 1179656 | tf_op jit(solution)/shard_map/ppermute | solution.py:453
  60.3 20.0 %collective-permute-start.6 = (bf16[128,1536]{1,0:T(8,128)(2,1)S(1)}, bf16[128,1536]{1,0:T(8,128)(2,1)S(1)}, u32[]{:S(2)}, u32[]{:S(2)}) collective-permute-start(bf16[128,1536]{1,0:T(8,128)(2,1)S(1)} %get-tuple-element.59.refs_0_), channel_id=1, source_target_pairs={{0,1},{1,3},{3,2},{2,0},{4,5},{5,7},{7,6},{6,4},{8,9},{9,11},{11,1... | collective-permute-start | bytes 1179656 | tf_op jit(solution)/shard_map/ppermute | solution.py:453
  69.4 20.7 %collective-permute-start.15 = (bf16[128,1536]{1,0:T(8,128)(2,1)S(1)}, bf16[128,1536]{1,0:T(8,128)(2,1)S(1)}, u32[]{:S(2)}, u32[]{:S(2)}) collective-permute-start(bf16[128,1536]{1,0:T(8,128)(2,1)S(1)} %multiply_convert_fusion.refs_3_.refs_0_), channel_id=1, source_target_pairs={{0,1},{1,3},{3,2},{2,0},{4,5},{5,7},{7,6},{6,4},{8,9},{9,11},{11,1... | collective-permute-start | bytes 1179656 | tf_op jit(solution)/shard_map/ppermute | solution.py:453
  80.2 16.5 %collective-permute-start.13 = (bf16[128,1536]{1,0:T(8,128)(2,1)S(1)}, bf16[128,1536]{1,0:T(8,128)(2,1)S(1)}, u32[]{:S(2)}, u32[]{:S(2)}) collective-permute-start(bf16[128,1536]{1,0:T(8,128)(2,1)S(1)} %collective-permute-done.6.refs_0_), channel_id=1, source_target_pairs={{0,1},{1,3},{3,2},{2,0},{4,5},{5,7},{7,6},{6,4},{8,9},{9,11},{11,1... | collective-permute-start | bytes 1179656 | tf_op jit(solution)/shard_map/ppermute | solution.py:453
  90.1 14.7 %collective-permute-start.16 = (bf16[128,1536]{1,0:T(8,128)(2,1)S(1)}, bf16[128,1536]{1,0:T(8,128)(2,1)S(1)}, u32[]{:S(2)}, u32[]{:S(2)}) collective-permute-start(bf16[128,1536]{1,0:T(8,128)(2,1)S(1)} %collective-permute-done.15.refs_0_), channel_id=1, source_target_pairs={{0,1},{1,3},{3,2},{2,0},{4,5},{5,7},{7,6},{6,4},{8,9},{9,11},{11,1... | collective-permute-start | bytes 1179656 | tf_op jit(solution)/shard_map/ppermute | solution.py:453
  96.7 16.7 %collective-permute-start.14 = (bf16[128,1536]{1,0:T(8,128)(2,1)S(1)}, bf16[128,1536]{1,0:T(8,128)(2,1)S(1)}, u32[]{:S(2)}, u32[]{:S(2)}) collective-permute-start(bf16[128,1536]{1,0:T(8,128)(2,1)S(1)} %collective-permute-done.13.refs_0_), channel_id=1, source_target_pairs={{0,1},{1,3},{3,2},{2,0},{4,5},{5,7},{7,6},{6,4},{8,9},{9,11},{11,1... | collective-permute-start | bytes 1179656 | tf_op jit(solution)/shard_map/ppermute | solution.py:453
  104.8 12.9 %collective-permute-start.19 = (bf16[128,1536]{1,0:T(8,128)(2,1)S(1)}, bf16[128,1536]{1,0:T(8,128)(2,1)S(1)}, u32[]{:S(2)}, u32[]{:S(2)}) collective-permute-start(bf16[128,1536]{1,0:T(8,128)(2,1)S(1)} %collective-permute-done.16.refs_0_), channel_id=1, source_target_pairs={{0,1},{1,3},{3,2},{2,0},{4,5},{5,7},{7,6},{6,4},{8,9},{9,11},{11,1... | collective-permute-start | bytes 1179656 | tf_op jit(solution)/shard_map/ppermute | solution.py:453
  113.4 4.1 %copy-start.1 = (bf16[2048]{0:T(1024)(128)(2,1)S(1)}, bf16[2048]{0:T(1024)(128)(2,1)}, u32[]{:S(2)}) copy-start(bf16[2048]{0:T(1024)(128)(2,1)} %param.14) | copy-start | bytes 12292
  117.4 2.6 %collective-permute-start.17 = (bf16[64,2048]{1,0:T(8,128)(2,1)S(1)}, bf16[64,2048]{1,0:T(8,128)(2,1)S(1)}, u32[]{:S(2)}, u32[]{:S(2)}) collective-permute-start(bf16[64,2048]{1,0:T(8,128)(2,1)S(1)} %get-tuple-element.90.after_ref), channel_id=1, source_target_pairs={{0,4},{4,0},{8,12},{12,8},{1,5},{5,1},{9,13},{13,9},{2,6},{6,2},{1... | collective-permute-start | bytes 786440 | tf_op jit(solution)/shard_map/ppermute | solution.py:446
  119.7 1.8 %collective-permute-start.20 = (bf16[64,2048]{1,0:T(8,128)(2,1)S(1)}, bf16[64,2048]{1,0:T(8,128)(2,1)S(1)}, u32[]{:S(2)}, u32[]{:S(2)}) collective-permute-start(bf16[64,2048]{1,0:T(8,128)(2,1)S(1)} %get-tuple-element.94), channel_id=1, source_target_pairs={{0,4},{4,0},{8,12},{12,8},{1,5},{5,1},{9,13},{13,9},{2,6},{6,2},{1... | collective-permute-start | bytes 786440 | tf_op jit(solution)/shard_map/ppermute | solution.py:446
  120.1 6.8 %collective-permute-start.18 = (bf16[32,2048]{1,0:T(8,128)(2,1)S(1)}, bf16[32,2048]{1,0:T(8,128)(2,1)S(1)}, u32[]{:S(2)}, u32[]{:S(2)}) collective-permute-start(bf16[32,2048]{1,0:T(8,128)(2,1)S(1)} %slice.33), channel_id=1, source_target_pairs={{0,8},{4,12},{8,0},{12,4},{1,9},{5,13},{9,1},{13,5},{2,10},{6,14},... | collective-permute-start | bytes 393224 | tf_op jit(solution)/shard_map/ppermute | solution.py:446
  121.6 7.0 %collective-permute-start.21 = (bf16[32,2048]{1,0:T(8,128)(2,1)S(1)}, bf16[32,2048]{1,0:T(8,128)(2,1)S(1)}, u32[]{:S(2)}, u32[]{:S(2)}) collective-permute-start(bf16[32,2048]{1,0:T(8,128)(2,1)S(1)} %slice.32.refs_4_), channel_id=1, source_target_pairs={{0,8},{4,12},{8,0},{12,4},{1,9},{5,13},{9,1},{13,5},{2,10},{6,14},... | collective-permute-start | bytes 393224 | tf_op jit(solution)/shard_map/ppermute | solution.py:446

commit v2 on v1

--- a/solution.py
+++ b/solution.py
@@ -18,7 +18,7 @@
 DOWN_UNROLL = 3
 GRADIENT_UNROLL = 2
 KEEP_UP = (0, 3)
-KEEP_DOWN = (0, 3)
+KEEP_DOWN = (0, 2, 3)
 
 
 def gelu_value(argument):

time: 130 us -> 130 us (level)
  waiting for transfers between devices: 16.8 us -> 20.8 us
  Pallas kernels: 80.3 us -> 76.9 us
    ppermute x12, waiting for transfers between devices: 13.9 us -> 17.7 us  [passed_on(): return lax.ppermute(block, 'mp', ring)]
    pallas_call x16, Pallas kernels: 77.7 us -> 74.3 us  [call(): pl.pallas_call(kernel, in_specs=operands.specs, out_specs=[spec for _, sp...]
  transfers between devices with their start and end apart: 22 -> 22, of which waited for: 11 -> 14; matrix products, arithmetic and copies ran while one was open for 3% -> 3% of each run, Pallas kernels for 62% -> 59%
where the time goes in v2:
time: 130 us; the launch traced here: 129 us
  Pallas kernels  76.9 us (59%)
  starting transfers between devices  26.2 us (20%)
  waiting for transfers between devices  20.8 us (16%)
  local copies, waits for them, and re-layouts  2.78 us (2%)
  other arithmetic  1.61 us (1%)
    pallas_call x16, Pallas kernels, call(): pl.pallas_call(kernel, in_specs=operands.specs, out_specs=[spec for _, sp...  74.3 us
    ppermute x12, starting transfers between devices, passed_on(): return lax.ppermute(block, 'mp', ring)  18.2 us
    ppermute x12, waiting for transfers between devices, passed_on(): return lax.ppermute(block, 'mp', ring)  17.7 us
    ppermute x2, starting transfers between devices, first_exchange(): return [own_rows, lax.ppermute(own_rows, 'hidden', partner_pairs(bits[0]))]  4.77 us
    ppermute x4, starting transfers between devices, scattered_sum(): lax.ppermute(sent, 'hidden', partner_pairs(bit)).astype(jnp.float32)  2.78 us
  transfers between devices with their start and end apart: 22, of which 14 were waited for; matrix products, arithmetic and copies ran while one was open for 3% of the time, Pallas kernels for 59%

profile of v2, /device:TPU:0, one launch (start us, length us, event | category | flops | bytes accessed | tf_op | source)
XLA Modules:
  0.0 129.3 jit_solution(2601589107573892253)
XLA Ops:
  0.6 0.0 copy-start
  0.6 3.0 %collective-permute-start = (bf16[32,2048]{1,0:T(8,128)(2,1)}, bf16[32,2048]{1,0:T(8,128)(2,1)S(1)}, u32[]{:S(2)}, u32[]{:S(2)}) collective-permute-start(bf16[32,2048]{1,0:T(8,128)(2,1)} %refs_0_.1), channel_id=1, source_target_pairs={{0,8},{4,12},{8,0},{12,4},{1,9},{5,13},{9,1},{13,5},{2,10},{6,14},... | collective-permute-start | bytes 393224 | tf_op jit(solution)/shard_map/ppermute | solution.py:436
  3.7 0.8 dynamic-slice.3
  4.5 0.8 copy.20
  5.2 0.2 broadcast_in_dim.8
  5.4 0.1 reshape_reshape.3.refs_5_.refs_2_.refs_3_
  5.5 0.9 broadcast_in_dim.7
  6.3 0.1 copy.23
  6.5 0.9 collective-permute-done.refs_1_
  7.4 0.0 collective-permute-start.2
  7.4 1.7 %collective-permute-start.7 = (bf16[32,2048]{1,0:T(8,128)(2,1)}, bf16[32,2048]{1,0:T(8,128)(2,1)S(1)}, u32[]{:S(2)}, u32[]{:S(2)}) collective-permute-start(bf16[32,2048]{1,0:T(8,128)(2,1)} %refs_0_.2), channel_id=1, source_target_pairs={{0,8},{4,12},{8,0},{12,4},{1,9},{5,13},{9,1},{13,5},{2,10},{6,14},... | collective-permute-start | bytes 393224 | tf_op jit(solution)/shard_map/ppermute | solution.py:436
  9.1 3.7 %up_share.4 = (bf16[128,1536]{1,0:T(8,128)(2,1)S(1)}, bf16[128,2048]{1,0:T(8,128)(2,1)S(1)}) custom-call(s32[1]{0:T(128)} %bitcast.1.block_ref, bf16[32,2048]{1,0:T(8,128)(2,1)} %refs_0_.1, bf16[32,2048]{1,0:T(8,128)(2,1)S(1)} %collective-permute-done.refs_1_, bf16[32,2048]{1,0:T(8,128)(2,1)S(1)} %collective-permute-done.1.refs_2_, ...), custom_call_target="tpu_custom_call" | custom-call | flops 2415919104 | bytes 18874368 | tf_op jit(solution)/shard_map/up_share/pallas_call | solution.py:271
  12.9 1.6 %collective-permute-start.3 = (bf16[128,1536]{1,0:T(8,128)(2,1)S(1)}, bf16[128,1536]{1,0:T(8,128)(2,1)S(1)}, u32[]{:S(2)}, u32[]{:S(2)}) collective-permute-start(bf16[128,1536]{1,0:T(8,128)(2,1)S(1)} %get-tuple-element.57), channel_id=1, source_target_pairs={{0,1},{1,3},{3,2},{2,0},{4,5},{5,7},{7,6},{6,4},{8,9},{9,11},{11,1... | collective-permute-start | bytes 1179656 | tf_op jit(solution)/shard_map/ppermute | solution.py:453
  14.5 0.0 collective-permute-start.8
  14.5 0.5 collective-permute-start.9
  15.0 0.8 collective-permute-done.8.refs_2_
  15.8 0.2 collective-permute-done.9.refs_3_
  16.0 4.4 %down_share.4 = (bf16[128,1536]{1,0:T(8,128)(2,1)S(1)}, bf16[128,2048]{1,0:T(8,128)(2,1)S(1)}) custom-call(s32[1]{0:T(128)} %bitcast.1.block_ref, bf16[32,2048]{1,0:T(8,128)(2,1)} %refs_0_.2, bf16[32,2048]{1,0:T(8,128)(2,1)S(1)} %collective-permute-done.7.refs_1_, bf16[32,2048]{1,0:T(8,128)(2,1)S(1)} %collective-permute-done.8.refs_2_, ...), custom_call_target="tpu_custom_call" | custom-call | flops 2415919104 | bytes 18874368 | tf_op jit(solution)/shard_map/down_share/pallas_call | solution.py:271
  20.5 2.6 %collective-permute-start.10 = (bf16[128,1536]{1,0:T(8,128)(2,1)S(1)}, bf16[128,1536]{1,0:T(8,128)(2,1)S(1)}, u32[]{:S(2)}, u32[]{:S(2)}) collective-permute-start(bf16[128,1536]{1,0:T(8,128)(2,1)S(1)} %get-tuple-element.68), channel_id=1, source_target_pairs={{0,1},{1,3},{3,2},{2,0},{4,5},{5,7},{7,6},{6,4},{8,9},{9,11},{11,1... | collective-permute-start | bytes 1179656 | tf_op jit(solution)/shard_map/ppermute | solution.py:453
  23.1 2.6 %collective-permute-done.3.refs_3_ = bf16[128,1536]{1,0:T(8,128)(2,1)S(1)} collective-permute-done((bf16[128,1536]{1,0:T(8,128)(2,1)S(1)}, bf16[128,1536]{1,0:T(8,128)(2,1)S(1)}, u32[]{:S(2)}, u32[]{:S(2)}) %collective-permute-start.3) | collective-permute-done | bytes 393248 | tf_op jit(solution)/shard_map/ppermute | solution.py:453
  25.7 3.8 %up_share.5 = bf16[128,1536]{1,0:T(8,128)(2,1)S(1)} custom-call(s32[1]{0:T(128)} %bitcast.2.block_ref, bf16[128,2048]{1,0:T(8,128)(2,1)S(1)} %get-tuple-element.56.refs_0_, bf16[2048,6144]{1,0:T(8,128)(2,1)} %refs_2_.5, f32[16,6144]{1,0:T(8,128)S(1)} %bitcast.10, bf16[128,1536]{1,0:T(8,128)(2,1)S(1)} %collective-permute-done.3.refs_3_), custom_call_target="tpu_custom_call" | custom-call | flops 2415919104 | bytes 18874368 | tf_op jit(solution)/shard_map/up_share/pallas_call | solution.py:271
  29.5 0.9 collective-permute-start.4
  30.4 3.7 %collective-permute-done.10.refs_3_ = bf16[128,1536]{1,0:T(8,128)(2,1)S(1)} collective-permute-done((bf16[128,1536]{1,0:T(8,128)(2,1)S(1)}, bf16[128,1536]{1,0:T(8,128)(2,1)S(1)}, u32[]{:S(2)}, u32[]{:S(2)}) %collective-permute-start.10) | collective-permute-done | bytes 393248 | tf_op jit(solution)/shard_map/ppermute | solution.py:453
  34.1 4.6 %down_share.6 = (bf16[128,1536]{1,0:T(8,128)(2,1)S(1)}, bf16[1536,2048]{1,0:T(8,128)(2,1)S(1)}) custom-call(s32[1]{0:T(128)} %bitcast.2.block_ref, bf16[128,2048]{1,0:T(8,128)(2,1)S(1)} %get-tuple-element.64.refs_0_.refs_1_, bf16[6144,2048]{1,0:T(8,128)(2,1)} %refs_2_.3, f32[4,12,2048]{2,1,0:T(8,128)S(1)} %reshape_reshape.3.refs_5_.refs_2_.refs_3_, ...), custom_call_target="tpu_custom_call" | custom-call | flops 2415919104 | bytes 18874368 | tf_op jit(solution)/shard_map/down_share/pallas_call | solution.py:271
  38.7 1.0 collective-permute-start.11
  39.7 2.9 %collective-permute-done.4.refs_3_ = bf16[128,1536]{1,0:T(8,128)(2,1)S(1)} collective-permute-done((bf16[128,1536]{1,0:T(8,128)(2,1)S(1)}, bf16[128,1536]{1,0:T(8,128)(2,1)S(1)}, u32[]{:S(2)}, u32[]{:S(2)}) %collective-permute-start.4) | collective-permute-done | bytes 393248 | tf_op jit(solution)/shard_map/ppermute | solution.py:453
  42.5 3.8 %up_share.6 = (bf16[128,1536]{1,0:T(8,128)(2,1)S(1)}, bf16[2048,128]{1,0:T(8,128)(2,1)S(1)}, bf16[2048,1536]{1,0:T(8,128)(2,1)S(1)}) custom-call(s32[1]{0:T(128)} %bitcast.block_ref, bf16[128,2048]{1,0:T(8,128)(2,1)S(1)} %get-tuple-element.56.refs_0_, bf16[2048,6144]{1,0:T(8,128)(2,1)} %refs_2_.5, f32[16,6144]{1,0:T(8,128)S(1)} %bitcast.11, ...), custom_call_target="tpu_custom_call" | custom-call | flops 2415919104 | bytes 18874368 | tf_op jit(solution)/shard_map/up_share/pallas_call | solution.py:271
  46.4 1.0 collective-permute-start.5
  47.4 3.6 %up_share.7 = (bf16[128,1536]{1,0:T(8,128)(2,1)S(1)}, bf16[2048,1536]{1,0:T(8,128)(2,1)S(1)}) custom-call(s32[1]{0:T(128)} %bitcast.3.block_ref, bf16[128,2048]{1,0:T(8,128)(2,1)S(1)} %get-tuple-element.56.refs_0_, bf16[2048,6144]{1,0:T(8,128)(2,1)} %refs_2_.5, f32[16,6144]{1,0:T(8,128)S(1)} %bitcast.12), custom_call_target="tpu_custom_call" | custom-call | flops 2415919104 | bytes 18874368 | tf_op jit(solution)/shard_map/up_share/pallas_call | solution.py:271
  51.0 0.7 collective-permute-done.11.refs_3_
  51.7 4.6 %down_share.7 = (bf16[128,1536]{1,0:T(8,128)(2,1)S(1)}, bf16[1536,2048]{1,0:T(8,128)(2,1)S(1)}) custom-call(s32[1]{0:T(128)} %bitcast.block_ref, bf16[128,2048]{1,0:T(8,128)(2,1)S(1)} %get-tuple-element.64.refs_0_.refs_1_, bf16[6144,2048]{1,0:T(8,128)(2,1)} %refs_2_.3, f32[4,12,2048]{2,1,0:T(8,128)S(1)} %reshape_reshape.3.refs_5_.refs_2_.refs_3_, ...), custom_call_target="tpu_custom_call" | custom-call | flops 2415919104 | bytes 18874368 | tf_op jit(solution)/shard_map/down_share/pallas_call | solution.py:271
  56.3 2.7 %collective-permute-start.12 = (bf16[128,1536]{1,0:T(8,128)(2,1)S(1)}, bf16[128,1536]{1,0:T(8,128)(2,1)S(1)}, u32[]{:S(2)}, u32[]{:S(2)}) collective-permute-start(bf16[128,1536]{1,0:T(8,128)(2,1)S(1)} %get-tuple-element.70), channel_id=1, source_target_pairs={{0,1},{1,3},{3,2},{2,0},{4,5},{5,7},{7,6},{6,4},{8,9},{9,11},{11,1... | collective-permute-start | bytes 1179656 | tf_op jit(solution)/shard_map/ppermute | solution.py:453
  59.0 0.6 collective-permute-done.5.sum_ref
  59.6 0.7 activation.1
  60.3 1.4 %collective-permute-start.6 = (bf16[128,1536]{1,0:T(8,128)(2,1)S(1)}, bf16[128,1536]{1,0:T(8,128)(2,1)S(1)}, u32[]{:S(2)}, u32[]{:S(2)}) collective-permute-start(bf16[128,1536]{1,0:T(8,128)(2,1)S(1)} %get-tuple-element.61.refs_0_), channel_id=1, source_target_pairs={{0,1},{1,3},{3,2},{2,0},{4,5},{5,7},{7,6},{6,4},{8,9},{9,11},{11,1... | collective-permute-start | bytes 1179656 | tf_op jit(solution)/shard_map/ppermute | solution.py:453
  61.7 4.3 %down_share.5 = (bf16[128,1536]{1,0:T(8,128)(2,1)S(1)}, bf16[1536,2048]{1,0:T(8,128)(2,1)S(1)}) custom-call(s32[1]{0:T(128)} %bitcast.3.block_ref, bf16[128,2048]{1,0:T(8,128)(2,1)S(1)} %get-tuple-element.64.refs_0_.refs_1_, bf16[6144,2048]{1,0:T(8,128)(2,1)} %refs_2_.3, f32[4,12,2048]{2,1,0:T(8,128)S(1)} %reshape_reshape.3.refs_5_.refs_2_.refs_3_), custom_call_target="tpu_custom_call" | custom-call | flops 2415919104 | bytes 18874368 | tf_op jit(solution)/shard_map/down_share/pallas_call | solution.py:271
  66.0 3.3 %collective-permute-done.12 = bf16[128,1536]{1,0:T(8,128)(2,1)S(1)} collective-permute-done((bf16[128,1536]{1,0:T(8,128)(2,1)S(1)}, bf16[128,1536]{1,0:T(8,128)(2,1)S(1)}, u32[]{:S(2)}, u32[]{:S(2)}) %collective-permute-start.12) | collective-permute-done | bytes 393248 | tf_op jit(solution)/shard_map/ppermute | solution.py:453
  69.3 0.1 multiply_convert_fusion.refs_3_.refs_0_
  69.4 2.0 %collective-permute-start.15 = (bf16[128,1536]{1,0:T(8,128)(2,1)S(1)}, bf16[128,1536]{1,0:T(8,128)(2,1)S(1)}, u32[]{:S(2)}, u32[]{:S(2)}) collective-permute-start(bf16[128,1536]{1,0:T(8,128)(2,1)S(1)} %multiply_convert_fusion.refs_3_.refs_0_), channel_id=1, source_target_pairs={{0,1},{1,3},{3,2},{2,0},{4,5},{5,7},{7,6},{6,4},{8,9},{9,11},{11,1... | collective-permute-start | bytes 1179656 | tf_op jit(solution)/shard_map/ppermute | solution.py:453
  71.4 4.0 %down_gradient.4 = (f32[128,2048]{1,0:T(8,128)S(1)}, bf16[6144,2048]{1,0:T(8,128)(2,1)}) custom-call(s32[1]{0:T(128)} %bitcast.3.block_ref, bf16[128,1536]{1,0:T(8,128)(2,1)S(1)} %get-tuple-element.61.refs_0_, bf16[128,2048]{1,0:T(8,128)(2,1)S(1)} %get-tuple-element.64.refs_0_.refs_1_, bf16[1536,2048]{1,0:T(8,128)(2,1)S(1)} %get-tuple-element.66.refs_2_, ...), custom_call_target="tpu_custom_call" | custom-call | flops 4831838208 | bytes 37748736 | tf_op jit(solution)/shard_map/down_gradient/pallas_call | solution.py:271
  75.4 4.8 %up_gradient.4 = (f32[2048,128]{1,0:T(8,128)S(1)}, bf16[2048,6144]{1,0:T(8,128)(2,1)}, f32[1,6144]{1,0:T(1,128)S(1)}) custom-call(s32[1]{0:T(128)} %bitcast.3.block_ref, bf16[128,1536]{1,0:T(8,128)(2,1)S(1)} %multiply_convert_fusion.refs_3_.refs_0_, bf16[2048,128]{1,0:T(8,128)(2,1)S(1)} %get-tuple-element.76.refs_1_, ...), custom_call_target="tpu_custom_call" | custom-call | flops 4831838208 | bytes 37748736 | tf_op jit(solution)/shard_map/up_gradient/pallas_call | solution.py:271
  80.2 2.5 %collective-permute-start.13 = (bf16[128,1536]{1,0:T(8,128)(2,1)S(1)}, bf16[128,1536]{1,0:T(8,128)(2,1)S(1)}, u32[]{:S(2)}, u32[]{:S(2)}) collective-permute-start(bf16[128,1536]{1,0:T(8,128)(2,1)S(1)} %collective-permute-done.6.refs_0_), channel_id=1, source_target_pairs={{0,1},{1,3},{3,2},{2,0},{4,5},{5,7},{7,6},{6,4},{8,9},{9,11},{11,1... | collective-permute-start | bytes 1179656 | tf_op jit(solution)/shard_map/ppermute | solution.py:453
  82.8 7.4 %down_gradient.5 = (f32[128,2048]{1,0:T(8,128)S(1)}, bf16[6144,2048]{1,0:T(8,128)(2,1)}) custom-call(s32[1]{0:T(128)} %bitcast.1.block_ref, bf16[128,1536]{1,0:T(8,128)(2,1)S(1)} %collective-permute-done.6.refs_0_, bf16[128,2048]{1,0:T(8,128)(2,1)S(1)} %get-tuple-element.64.refs_0_.refs_1_, ...), custom_call_target="tpu_custom_call", output_to_operand_aliasing={{1}: (6, {})} | custom-call | flops 4831838208 | bytes 37748736 | tf_op jit(solution)/shard_map/down_gradient/pallas_call | solution.py:271
  90.2 0.1 collective-permute-start.16
  90.2 6.5 %up_gradient.5 = (f32[2048,128]{1,0:T(8,128)S(1)}, bf16[2048,6144]{1,0:T(8,128)(2,1)}, f32[1,6144]{1,0:T(1,128)S(1)}) custom-call(s32[1]{0:T(128)} %bitcast.1.block_ref, bf16[128,1536]{1,0:T(8,128)(2,1)S(1)} %collective-permute-done.15.refs_0_, bf16[2048,128]{1,0:T(8,128)(2,1)S(1)} %get-tuple-element.76.refs_1_, ...), custom_call_target="tpu_custom_call", output_to_operand_aliasing={{1}: (6, {})} | custom-call | flops 4831838208 | bytes 37748736 | tf_op jit(solution)/shard_map/up_gradient/pallas_call | solution.py:271
  96.7 0.7 collective-permute-start.14
  97.5 4.0 %down_gradient.6 = (f32[128,2048]{1,0:T(8,128)S(1)}, bf16[6144,2048]{1,0:T(8,128)(2,1)}) custom-call(s32[1]{0:T(128)} %bitcast.2.block_ref, bf16[128,1536]{1,0:T(8,128)(2,1)S(1)} %collective-permute-done.13.refs_0_, bf16[128,2048]{1,0:T(8,128)(2,1)S(1)} %get-tuple-element.64.refs_0_.refs_1_, ...), custom_call_target="tpu_custom_call", output_to_operand_aliasing={{1}: (5, {})} | custom-call | flops 4831838208 | bytes 37748736 | tf_op jit(solution)/shard_map/down_gradient/pallas_call | solution.py:271
  101.5 1.7 %collective-permute-done.16.refs_0_ = bf16[128,1536]{1,0:T(8,128)(2,1)S(1)} collective-permute-done((bf16[128,1536]{1,0:T(8,128)(2,1)S(1)}, bf16[128,1536]{1,0:T(8,128)(2,1)S(1)}, u32[]{:S(2)}, u32[]{:S(2)}) %collective-permute-start.16) | collective-permute-done | bytes 393248 | tf_op jit(solution)/shard_map/ppermute | solution.py:453
  103.2 1.6 %collective-permute-start.19 = (bf16[128,1536]{1,0:T(8,128)(2,1)S(1)}, bf16[128,1536]{1,0:T(8,128)(2,1)S(1)}, u32[]{:S(2)}, u32[]{:S(2)}) collective-permute-start(bf16[128,1536]{1,0:T(8,128)(2,1)S(1)} %collective-permute-done.16.refs_0_), channel_id=1, source_target_pairs={{0,1},{1,3},{3,2},{2,0},{4,5},{5,7},{7,6},{6,4},{8,9},{9,11},{11,1... | collective-permute-start | bytes 1179656 | tf_op jit(solution)/shard_map/ppermute | solution.py:453
  104.7 6.5 %up_gradient.6 = (f32[2048,128]{1,0:T(8,128)S(1)}, bf16[2048,6144]{1,0:T(8,128)(2,1)}, f32[1,6144]{1,0:T(1,128)S(1)}) custom-call(s32[1]{0:T(128)} %bitcast.2.block_ref, bf16[128,1536]{1,0:T(8,128)(2,1)S(1)} %collective-permute-done.16.refs_0_, bf16[2048,128]{1,0:T(8,128)(2,1)S(1)} %get-tuple-element.76.refs_1_, ...), custom_call_target="tpu_custom_call", output_to_operand_aliasing={{1}: (6, {})} | custom-call | flops 4831838208 | bytes 37748736 | tf_op jit(solution)/shard_map/up_gradient/pallas_call | solution.py:271
  111.2 0.0 copy-start.1
  111.3 0.3 collective-permute-done.14.refs_0_
  111.6 4.0 %down_gradient.7 = (f32[64,2048]{1,0:T(8,128)S(1)}, bf16[64,2048]{1,0:T(8,128)(2,1)S(1)}, bf16[6144,2048]{1,0:T(8,128)(2,1)}) custom-call(s32[1]{0:T(128)} %bitcast.block_ref, bf16[128,1536]{1,0:T(8,128)(2,1)S(1)} %collective-permute-done.14.refs_0_, bf16[128,2048]{1,0:T(8,128)(2,1)S(1)} %get-tuple-element.64.refs_0_.refs_1_, ...), custom_call_target="tpu_custom_call", output_to_operand_aliasing={{2}: (5, {})} | custom-call | flops 4831838208 | bytes 37748736 | tf_op jit(solution)/shard_map/down_gradient/pallas_call | solution.py:271
  115.6 0.1 collective-permute-start.17
  115.7 2.0 %collective-permute-done.19.act_ref.refs_0_ = bf16[128,1536]{1,0:T(8,128)(2,1)S(1)} collective-permute-done((bf16[128,1536]{1,0:T(8,128)(2,1)S(1)}, bf16[128,1536]{1,0:T(8,128)(2,1)S(1)}, u32[]{:S(2)}, u32[]{:S(2)}) %collective-permute-start.19) | collective-permute-done | bytes 393248 | tf_op jit(solution)/shard_map/ppermute | solution.py:453
  117.7 1.9 %last_product.1 = (f32[64,2048]{1,0:T(8,128)S(1)}, bf16[64,2048]{1,0:T(8,128)(2,1)S(1)}) custom-call(bf16[128,1536]{1,0:T(8,128)(2,1)S(1)} %collective-permute-done.19.act_ref.refs_0_, bf16[2048,1536]{1,0:T(8,128)(2,1)S(1)} %get-tuple-element.96.weights_ref, f32[2048,128]{1,0:T(8,128)S(1)} %get-tuple-element.92.refs_5_.total_in, ...), custom_call_target="tpu_custom_call" | custom-call | flops 2415919104 | bytes 18874368 | tf_op jit(solution)/shard_map/last_product/pallas_call | solution.py:410
  119.7 0.1 collective-permute-start.20
  119.8 1.3 %collective-permute-start.18 = (bf16[32,2048]{1,0:T(8,128)(2,1)S(1)}, bf16[32,2048]{1,0:T(8,128)(2,1)S(1)}, u32[]{:S(2)}, u32[]{:S(2)}) collective-permute-start(bf16[32,2048]{1,0:T(8,128)(2,1)S(1)} %slice.33), channel_id=1, source_target_pairs={{0,8},{4,12},{8,0},{12,4},{1,9},{5,13},{9,1},{13,5},{2,10},{6,14},... | collective-permute-start | bytes 393224 | tf_op jit(solution)/shard_map/ppermute | solution.py:446
  121.2 0.1 collective-permute-done.20
  121.3 1.3 %collective-permute-start.21 = (bf16[32,2048]{1,0:T(8,128)(2,1)S(1)}, bf16[32,2048]{1,0:T(8,128)(2,1)S(1)}, u32[]{:S(2)}, u32[]{:S(2)}) collective-permute-start(bf16[32,2048]{1,0:T(8,128)(2,1)S(1)} %slice.32.refs_4_), channel_id=1, source_target_pairs={{0,8},{4,12},{8,0},{12,4},{1,9},{5,13},{9,1},{13,5},{2,10},{6,14},... | collective-permute-start | bytes 393224 | tf_op jit(solution)/shard_map/ppermute | solution.py:446
  122.7 4.2 %up_gradient.7 = (bf16[2048,6144]{1,0:T(8,128)(2,1)}, f32[1,6144]{1,0:T(1,128)}) custom-call(s32[1]{0:T(128)} %bitcast.block_ref, bf16[128,1536]{1,0:T(8,128)(2,1)S(1)} %collective-permute-done.19.act_ref.refs_0_, bf16[2048,128]{1,0:T(8,128)(2,1)S(1)} %get-tuple-element.76.refs_1_, ...), custom_call_target="tpu_custom_call", output_to_operand_aliasing={{0}: (3, {})} | custom-call | flops 4831838208 | bytes 18874368 | tf_op jit(solution)/shard_map/up_gradient/pallas_call | solution.py:271
  126.9 0.7 fusion.2
  127.6 1.0 collective-permute-done.21
  128.6 0.7 fusion
  (17 shorter events, 0.2 us)
Async XLA Ops:
  0.6 13.9 %copy-start = (bf16[32,2048]{1,0:T(8,128)(2,1)S(1)}, bf16[32,2048]{1,0:T(8,128)(2,1)}, u32[]{:S(2)}) copy-start(bf16[32,2048]{1,0:T(8,128)(2,1)} %refs_0_.2) | copy-start | bytes 393220
  0.6 6.7 %collective-permute-start = (bf16[32,2048]{1,0:T(8,128)(2,1)}, bf16[32,2048]{1,0:T(8,128)(2,1)S(1)}, u32[]{:S(2)}, u32[]{:S(2)}) collective-permute-start(bf16[32,2048]{1,0:T(8,128)(2,1)} %refs_0_.1), channel_id=1, source_target_pairs={{0,8},{4,12},{8,0},{12,4},{1,9},{5,13},{9,1},{13,5},{2,10},{6,14},... | collective-permute-start | bytes 393224 | tf_op jit(solution)/shard_map/ppermute | solution.py:436
  3.7 5.5 %collective-permute-start.1 = (bf16[32,2048]{1,0:T(8,128)(2,1)}, bf16[32,2048]{1,0:T(8,128)(2,1)S(1)}, u32[]{:S(2)}, u32[]{:S(2)}) collective-permute-start(bf16[32,2048]{1,0:T(8,128)(2,1)} %refs_0_.1), channel_id=1, source_target_pairs={{0,4},{4,0},{8,12},{12,8},{1,5},{5,1},{9,13},{13,9},{2,6},{6,2},{1... | collective-permute-start | bytes 393224 | tf_op jit(solution)/shard_map/ppermute | solution.py:441
  7.4 1.7 %collective-permute-start.2 = (bf16[32,2048]{1,0:T(8,128)(2,1)S(1)}, bf16[32,2048]{1,0:T(8,128)(2,1)S(1)}, u32[]{:S(2)}, u32[]{:S(2)}) collective-permute-start(bf16[32,2048]{1,0:T(8,128)(2,1)S(1)} %collective-permute-done.refs_1_), channel_id=1, source_target_pairs={{0,4},{4,0},{8,12},{12,8},{1,5},{5,1},{9,13},{13,9},{2,6},{6,2},{1... | collective-permute-start | bytes 393224 | tf_op jit(solution)/shard_map/ppermute | solution.py:441
  7.4 7.1 %collective-permute-start.7 = (bf16[32,2048]{1,0:T(8,128)(2,1)}, bf16[32,2048]{1,0:T(8,128)(2,1)S(1)}, u32[]{:S(2)}, u32[]{:S(2)}) collective-permute-start(bf16[32,2048]{1,0:T(8,128)(2,1)} %refs_0_.2), channel_id=1, source_target_pairs={{0,8},{4,12},{8,0},{12,4},{1,9},{5,13},{9,1},{13,5},{2,10},{6,14},... | collective-permute-start | bytes 393224 | tf_op jit(solution)/shard_map/ppermute | solution.py:436
  12.9 12.8 %collective-permute-start.3 = (bf16[128,1536]{1,0:T(8,128)(2,1)S(1)}, bf16[128,1536]{1,0:T(8,128)(2,1)S(1)}, u32[]{:S(2)}, u32[]{:S(2)}) collective-permute-start(bf16[128,1536]{1,0:T(8,128)(2,1)S(1)} %get-tuple-element.57), channel_id=1, source_target_pairs={{0,1},{1,3},{3,2},{2,0},{4,5},{5,7},{7,6},{6,4},{8,9},{9,11},{11,1... | collective-permute-start | bytes 1179656 | tf_op jit(solution)/shard_map/ppermute | solution.py:453
  14.5 1.3 %collective-permute-start.8 = (bf16[32,2048]{1,0:T(8,128)(2,1)S(1)}, bf16[32,2048]{1,0:T(8,128)(2,1)S(1)}, u32[]{:S(2)}, u32[]{:S(2)}) collective-permute-start(bf16[32,2048]{1,0:T(8,128)(2,1)S(1)} %copy-done), channel_id=1, source_target_pairs={{0,4},{4,0},{8,12},{12,8},{1,5},{5,1},{9,13},{13,9},{2,6},{6,2},{1... | collective-permute-start | bytes 393224 | tf_op jit(solution)/shard_map/ppermute | solution.py:441
  14.5 1.5 %collective-permute-start.9 = (bf16[32,2048]{1,0:T(8,128)(2,1)S(1)}, bf16[32,2048]{1,0:T(8,128)(2,1)S(1)}, u32[]{:S(2)}, u32[]{:S(2)}) collective-permute-start(bf16[32,2048]{1,0:T(8,128)(2,1)S(1)} %collective-permute-done.7.refs_1_), channel_id=1, source_target_pairs={{0,4},{4,0},{8,12},{12,8},{1,5},{5,1},{9,13},{13,9},{2,6},{6,2},{1... | collective-permute-start | bytes 393224 | tf_op jit(solution)/shard_map/ppermute | solution.py:441
  20.5 13.6 %collective-permute-start.10 = (bf16[128,1536]{1,0:T(8,128)(2,1)S(1)}, bf16[128,1536]{1,0:T(8,128)(2,1)S(1)}, u32[]{:S(2)}, u32[]{:S(2)}) collective-permute-start(bf16[128,1536]{1,0:T(8,128)(2,1)S(1)} %get-tuple-element.68), channel_id=1, source_target_pairs={{0,1},{1,3},{3,2},{2,0},{4,5},{5,7},{7,6},{6,4},{8,9},{9,11},{11,1... | collective-permute-start | bytes 1179656 | tf_op jit(solution)/shard_map/ppermute | solution.py:453
  29.5 13.0 %collective-permute-start.4 = (bf16[128,1536]{1,0:T(8,128)(2,1)S(1)}, bf16[128,1536]{1,0:T(8,128)(2,1)S(1)}, u32[]{:S(2)}, u32[]{:S(2)}) collective-permute-start(bf16[128,1536]{1,0:T(8,128)(2,1)S(1)} %up_share.5), channel_id=1, source_target_pairs={{0,1},{1,3},{3,2},{2,0},{4,5},{5,7},{7,6},{6,4},{8,9},{9,11},{11,1... | collective-permute-start | bytes 1179656 | tf_op jit(solution)/shard_map/ppermute | solution.py:453
  38.7 13.0 %collective-permute-start.11 = (bf16[128,1536]{1,0:T(8,128)(2,1)S(1)}, bf16[128,1536]{1,0:T(8,128)(2,1)S(1)}, u32[]{:S(2)}, u32[]{:S(2)}) collective-permute-start(bf16[128,1536]{1,0:T(8,128)(2,1)S(1)} %get-tuple-element.69), channel_id=1, source_target_pairs={{0,1},{1,3},{3,2},{2,0},{4,5},{5,7},{7,6},{6,4},{8,9},{9,11},{11,1... | collective-permute-start | bytes 1179656 | tf_op jit(solution)/shard_map/ppermute | solution.py:453
  46.4 13.2 %collective-permute-start.5 = (bf16[128,1536]{1,0:T(8,128)(2,1)S(1)}, bf16[128,1536]{1,0:T(8,128)(2,1)S(1)}, u32[]{:S(2)}, u32[]{:S(2)}) collective-permute-start(bf16[128,1536]{1,0:T(8,128)(2,1)S(1)} %get-tuple-element.58), channel_id=1, source_target_pairs={{0,1},{1,3},{3,2},{2,0},{4,5},{5,7},{7,6},{6,4},{8,9},{9,11},{11,1... | collective-permute-start | bytes 1179656 | tf_op jit(solution)/shard_map/ppermute | solution.py:453
  56.3 13.0 %collective-permute-start.12 = (bf16[128,1536]{1,0:T(8,128)(2,1)S(1)}, bf16[128,1536]{1,0:T(8,128)(2,1)S(1)}, u32[]{:S(2)}, u32[]{:S(2)}) collective-permute-start(bf16[128,1536]{1,0:T(8,128)(2,1)S(1)} %get-tuple-element.70), channel_id=1, source_target_pairs={{0,1},{1,3},{3,2},{2,0},{4,5},{5,7},{7,6},{6,4},{8,9},{9,11},{11,1... | collective-permute-start | bytes 1179656 | tf_op jit(solution)/shard_map/ppermute | solution.py:453
  60.3 20.0 %collective-permute-start.6 = (bf16[128,1536]{1,0:T(8,128)(2,1)S(1)}, bf16[128,1536]{1,0:T(8,128)(2,1)S(1)}, u32[]{:S(2)}, u32[]{:S(2)}) collective-permute-start(bf16[128,1536]{1,0:T(8,128)(2,1)S(1)} %get-tuple-element.61.refs_0_), channel_id=1, source_target_pairs={{0,1},{1,3},{3,2},{2,0},{4,5},{5,7},{7,6},{6,4},{8,9},{9,11},{11,1... | collective-permute-start | bytes 1179656 | tf_op jit(solution)/shard_map/ppermute | solution.py:453
  69.4 20.7 %collective-permute-start.15 = (bf16[128,1536]{1,0:T(8,128)(2,1)S(1)}, bf16[128,1536]{1,0:T(8,128)(2,1)S(1)}, u32[]{:S(2)}, u32[]{:S(2)}) collective-permute-start(bf16[128,1536]{1,0:T(8,128)(2,1)S(1)} %multiply_convert_fusion.refs_3_.refs_0_), channel_id=1, source_target_pairs={{0,1},{1,3},{3,2},{2,0},{4,5},{5,7},{7,6},{6,4},{8,9},{9,11},{11,1... | collective-permute-start | bytes 1179656 | tf_op jit(solution)/shard_map/ppermute | solution.py:453
  80.2 16.5 %collective-permute-start.13 = (bf16[128,1536]{1,0:T(8,128)(2,1)S(1)}, bf16[128,1536]{1,0:T(8,128)(2,1)S(1)}, u32[]{:S(2)}, u32[]{:S(2)}) collective-permute-start(bf16[128,1536]{1,0:T(8,128)(2,1)S(1)} %collective-permute-done.6.refs_0_), channel_id=1, source_target_pairs={{0,1},{1,3},{3,2},{2,0},{4,5},{5,7},{7,6},{6,4},{8,9},{9,11},{11,1... | collective-permute-start | bytes 1179656 | tf_op jit(solution)/shard_map/ppermute | solution.py:453
  90.2 13.0 %collective-permute-start.16 = (bf16[128,1536]{1,0:T(8,128)(2,1)S(1)}, bf16[128,1536]{1,0:T(8,128)(2,1)S(1)}, u32[]{:S(2)}, u32[]{:S(2)}) collective-permute-start(bf16[128,1536]{1,0:T(8,128)(2,1)S(1)} %collective-permute-done.15.refs_0_), channel_id=1, source_target_pairs={{0,1},{1,3},{3,2},{2,0},{4,5},{5,7},{7,6},{6,4},{8,9},{9,11},{11,1... | collective-permute-start | bytes 1179656 | tf_op jit(solution)/shard_map/ppermute | solution.py:453
  96.7 14.9 %collective-permute-start.14 = (bf16[128,1536]{1,0:T(8,128)(2,1)S(1)}, bf16[128,1536]{1,0:T(8,128)(2,1)S(1)}, u32[]{:S(2)}, u32[]{:S(2)}) collective-permute-start(bf16[128,1536]{1,0:T(8,128)(2,1)S(1)} %collective-permute-done.13.refs_0_), channel_id=1, source_target_pairs={{0,1},{1,3},{3,2},{2,0},{4,5},{5,7},{7,6},{6,4},{8,9},{9,11},{11,1... | collective-permute-start | bytes 1179656 | tf_op jit(solution)/shard_map/ppermute | solution.py:453
  103.2 14.6 %collective-permute-start.19 = (bf16[128,1536]{1,0:T(8,128)(2,1)S(1)}, bf16[128,1536]{1,0:T(8,128)(2,1)S(1)}, u32[]{:S(2)}, u32[]{:S(2)}) collective-permute-start(bf16[128,1536]{1,0:T(8,128)(2,1)S(1)} %collective-permute-done.16.refs_0_), channel_id=1, source_target_pairs={{0,1},{1,3},{3,2},{2,0},{4,5},{5,7},{7,6},{6,4},{8,9},{9,11},{11,1... | collective-permute-start | bytes 1179656 | tf_op jit(solution)/shard_map/ppermute | solution.py:453
  111.2 4.4 %copy-start.1 = (bf16[2048]{0:T(1024)(128)(2,1)S(1)}, bf16[2048]{0:T(1024)(128)(2,1)}, u32[]{:S(2)}) copy-start(bf16[2048]{0:T(1024)(128)(2,1)} %param.14) | copy-start | bytes 12292
  115.6 4.2 %collective-permute-start.17 = (bf16[64,2048]{1,0:T(8,128)(2,1)S(1)}, bf16[64,2048]{1,0:T(8,128)(2,1)S(1)}, u32[]{:S(2)}, u32[]{:S(2)}) collective-permute-start(bf16[64,2048]{1,0:T(8,128)(2,1)S(1)} %get-tuple-element.94.after_ref), channel_id=1, source_target_pairs={{0,4},{4,0},{8,12},{12,8},{1,5},{5,1},{9,13},{13,9},{2,6},{6,2},{1... | collective-permute-start | bytes 786440 | tf_op jit(solution)/shard_map/ppermute | solution.py:446
  119.7 1.6 %collective-permute-start.20 = (bf16[64,2048]{1,0:T(8,128)(2,1)S(1)}, bf16[64,2048]{1,0:T(8,128)(2,1)S(1)}, u32[]{:S(2)}, u32[]{:S(2)}) collective-permute-start(bf16[64,2048]{1,0:T(8,128)(2,1)S(1)} %get-tuple-element.98), channel_id=1, source_target_pairs={{0,4},{4,0},{8,12},{12,8},{1,5},{5,1},{9,13},{13,9},{2,6},{6,2},{1... | collective-permute-start | bytes 786440 | tf_op jit(solution)/shard_map/ppermute | solution.py:446
  119.8 7.1 %collective-permute-start.18 = (bf16[32,2048]{1,0:T(8,128)(2,1)S(1)}, bf16[32,2048]{1,0:T(8,128)(2,1)S(1)}, u32[]{:S(2)}, u32[]{:S(2)}) collective-permute-start(bf16[32,2048]{1,0:T(8,128)(2,1)S(1)} %slice.33), channel_id=1, source_target_pairs={{0,8},{4,12},{8,0},{12,4},{1,9},{5,13},{9,1},{13,5},{2,10},{6,14},... | collective-permute-start | bytes 393224 | tf_op jit(solution)/shard_map/ppermute | solution.py:446
  121.3 7.3 %collective-permute-start.21 = (bf16[32,2048]{1,0:T(8,128)(2,1)S(1)}, bf16[32,2048]{1,0:T(8,128)(2,1)S(1)}, u32[]{:S(2)}, u32[]{:S(2)}) collective-permute-start(bf16[32,2048]{1,0:T(8,128)(2,1)S(1)} %slice.32.refs_4_), channel_id=1, source_target_pairs={{0,8},{4,12},{8,0},{12,4},{1,9},{5,13},{9,1},{13,5},{2,10},{6,14},... | collective-permute-start | bytes 393224 | tf_op jit(solution)/shard_map/ppermute | solution.py:446
